TPU v7x, 32 devices: a whole 2x2x4 slice. The times are simulated.
32 devices in a mesh: gx: 4 (over y, core), gy: 4 (over z), gz: 2 (over x).
Axes of the slice: x: 2, y: 2, z: 4, core: 2. Of those that a mesh axis runs over, the one named last changes fastest.
Arguments:
- particles: bfloat16 [4, 4, 2, 256, 512], P('gx', 'gy', 'gz'), may hold values from -6 to 6
- log_weight: bfloat16 [4, 4, 2, 256], P('gx', 'gy', 'gz'), may hold values from -4 to 296
- counts: int32 [4, 4, 2], P('gx', 'gy', 'gz'), may hold values from 1 to 256, as said below
- pattern: int32 [4, 4, 2, 6], P('gx', 'gy', 'gz'), may hold values from 0 to 1, as said below
- query_weight: bfloat16 [512, 512], replicated, may hold values from -0.25 to 0.25
- key_value_weight: bfloat16 [512, 1024], replicated, may hold values from -0.25 to 0.25
- output_weight: bfloat16 [512, 512], replicated, may hold values from -0.75 to 0.75
- baffle_store: bfloat16 [32, 1024, 1024], P(('gx', 'gy', 'gz')), may hold values from -6 to 6
- owner_device: int32 [1], replicated, may hold values from 0 to 31
- cotangent: bfloat16 [4, 4, 2, 256, 512], P('gx', 'gy', 'gz'), may hold values from -6 to 6
Outputs:
- update: bfloat16 [4, 4, 2, 256, 512], P('gx', 'gy', 'gz')
- grad_particles: bfloat16 [4, 4, 2, 256, 512], P('gx', 'gy', 'gz')
- grad_query: float32 [262144], P(('gx', 'gy', 'gz'))
- grad_key_value: float32 [524288], P(('gx', 'gy', 'gz'))
- grad_output: float32 [262144], P(('gx', 'gy', 'gz'))
- grad_baffle: float32 [1048576], P(('gx', 'gy', 'gz'))
Inputs may be any that keep to these rules, and one draw needn't show every extreme that they name: A patch holds its particles in its first counts slots. Patches whose z index lies below a drawn fill level hold 256 particles; the bottom layer always lies below it and the top layer never; the others hold 1 to 256. `pattern`: entries 2k and 2k+1 flag the lower and upper neighbour along grid dimension k (x, y, z). A flag is 0 where that neighbour lies outside the grid, and a patch flags a neighbour exactly when that neighbour flags it back. `owner_device`: the index of the device along gx+gy+gz, slowest axis first.
All inputs are finite; a program needn't handle non-finite values.
Results may differ from a plain program's by a relative error of at most 0.012.
The roundings to bfloat16 on the way count: a program that leaves them out, or rounds other values in their place, can miss the bound.
Values may be sent and summed in bfloat16 or wider, within the bound.
A program may use at most 128 MiB of HBM per device.

v0:
```python
import math

import jax
import jax.numpy as jnp
from jax import lax
from jax.sharding import PartitionSpec as P

D = 512
H = 8
HD = 64
P_SIZE = 256
NB = 1024


masked_bias = -1000000000.0


def padded(block, sides, width):
    for axis, dim in sides:
        count = lax.axis_size(axis)
        forward = [(i, i + 1) for i in range(count - 1)]
        backward = [(target, source) for source, target in forward]
        low = lax.ppermute(
            lax.slice_in_dim(block, block.shape[dim] - width, None, axis=dim), axis, forward
        )
        high = lax.ppermute(lax.slice_in_dim(block, 0, width, axis=dim), axis, backward)
        block = jnp.concatenate([low, block, high], axis=dim)
    return block


def broadcast(array, axis, root):
    mine = lax.axis_index(axis) == root
    return lax.psum(jnp.where(mine, array, jnp.zeros_like(array)), axis)


def layer_norm(values):
    row_mean = jnp.mean(values, axis=-1, keepdims=True)
    centered = values - row_mean
    inv_std = lax.rsqrt(jnp.mean(centered * centered, axis=-1, keepdims=True) + 1e-05)
    return (centered * inv_std, inv_std)


def layer_norm_back(grad_normed, normed, inv_std):
    first_mean = jnp.mean(grad_normed, axis=-1, keepdims=True)
    second_mean = jnp.mean(grad_normed * normed, axis=-1, keepdims=True)
    return inv_std * (grad_normed - first_mean - normed * second_mean)


def contract_last(left, right):
    return lax.dot_general(
        left, right, (((1,), (1,)), ((), ())), preferred_element_type=jnp.float32
    )


def contract_first(left, right):
    return lax.dot_general(
        left, right, (((0,), (0,)), ((), ())), preferred_element_type=jnp.float32
    )


def head_columns(block, head_index, offset):
    return lax.dynamic_slice_in_dim(block, offset + head_index * HD, HD, 1)


def merge_heads(stacked):
    return jnp.transpose(stacked, (1, 0, 2)).reshape(
        stacked.shape[1], stacked.shape[0] * stacked.shape[2]
    )


def take_faces(wide):
    return jnp.stack(
        [wide[0, 1, 1], wide[2, 1, 1], wide[1, 0, 1], wide[1, 2, 1], wide[1, 1, 0], wide[1, 1, 2]]
    )


def attend_forward(queries, all_keys, key_bias):
    score_scale = 1.0 / math.sqrt(HD)

    def attend_per_head(head_index):
        query_head = head_columns(queries, head_index, 0)
        key_head = head_columns(all_keys, head_index, 0)
        value_head = head_columns(all_keys, head_index, D)
        scores = contract_last(query_head, key_head) * score_scale + key_bias[None, :]
        top_score = jnp.max(scores, axis=1, keepdims=True)
        log_total = top_score[:, 0] + jnp.log(jnp.sum(jnp.exp(scores - top_score), axis=1))
        prob_low = jnp.exp(scores - log_total[:, None]).astype(jnp.bfloat16)
        return (jnp.dot(prob_low, value_head, preferred_element_type=jnp.float32), log_total)

    head_out, log_totals = lax.map(attend_per_head, jnp.arange(H, dtype=jnp.int32))
    return (merge_heads(head_out).astype(jnp.bfloat16), log_totals)


def query_back(queries, all_keys, key_bias, log_totals, attn, grad_attn):
    score_scale = 1.0 / math.sqrt(HD)
    baffle_start = all_keys.shape[0] - NB

    def query_per_head(head_index):
        query_head = head_columns(queries, head_index, 0)
        key_head = head_columns(all_keys, head_index, 0)
        value_head = head_columns(all_keys, head_index, D)
        attn_head = head_columns(attn, head_index, 0)
        grad_head = head_columns(grad_attn, head_index, 0)
        scores = contract_last(query_head, key_head) * score_scale + key_bias[None, :]
        prob_full = jnp.exp(scores - log_totals[head_index][:, None])
        prob_low = prob_full.astype(jnp.bfloat16)
        row_dot = jnp.sum(grad_head.astype(jnp.float32) * attn_head.astype(jnp.float32), axis=1)
        grad_prob = contract_last(grad_head, value_head)
        grad_score = (prob_full * (grad_prob - row_dot[:, None])).astype(jnp.bfloat16)
        grad_query_head = (
            jnp.dot(grad_score, key_head, preferred_element_type=jnp.float32) * score_scale
        )
        grad_bkey = contract_first(grad_score[:, baffle_start:], query_head) * score_scale
        grad_bvalue = contract_first(prob_low[:, baffle_start:], grad_head)
        return (grad_query_head, row_dot, grad_bkey, grad_bvalue)

    grad_heads, row_dots, bkey_heads, bvalue_heads = lax.map(
        query_per_head, jnp.arange(H, dtype=jnp.int32)
    )
    baffle_grad = jnp.concatenate([merge_heads(bkey_heads), merge_heads(bvalue_heads)], axis=1)
    return (merge_heads(grad_heads).astype(jnp.bfloat16), row_dots, baffle_grad)


def key_back(query_rows, grad_rows, total_rows, dot_rows, keep_rows, own_pairs, own_bias):
    score_scale = 1.0 / math.sqrt(HD)

    def key_per_head(head_index):
        query_head = head_columns(query_rows, head_index, 0)
        grad_head = head_columns(grad_rows, head_index, 0)
        key_head = head_columns(own_pairs, head_index, 0)
        value_head = head_columns(own_pairs, head_index, D)
        scores = contract_last(query_head, key_head) * score_scale + own_bias[None, :]
        shifted = jnp.where(
            keep_rows[:, None], scores - total_rows[head_index][:, None], masked_bias
        )
        prob_full = jnp.exp(shifted)
        grad_prob = contract_last(grad_head, value_head)
        grad_score = (prob_full * (grad_prob - dot_rows[head_index][:, None])).astype(jnp.bfloat16)
        grad_key_head = contract_first(grad_score, query_head) * score_scale
        grad_value_head = contract_first(prob_full.astype(jnp.bfloat16), grad_head)
        return (grad_key_head, grad_value_head)

    key_heads, value_heads = lax.map(key_per_head, jnp.arange(H, dtype=jnp.int32))
    return jnp.concatenate([merge_heads(key_heads), merge_heads(value_heads)], axis=1).astype(
        jnp.bfloat16
    )


def body(
    particles,
    log_weight,
    counts,
    pattern,
    query_weight,
    key_value_weight,
    output_weight,
    baffle_store,
    owner_device,
    cotangent,
):
    rows_in = particles[0, 0, 0].astype(jnp.float32)
    normed, inv_std = layer_norm(rows_in)
    normed_low = normed.astype(jnp.bfloat16)
    queries = jnp.dot(normed_low, query_weight, preferred_element_type=jnp.float32).astype(
        jnp.bfloat16
    )
    key_value = jnp.dot(normed_low, key_value_weight, preferred_element_type=jnp.float32).astype(
        jnp.bfloat16
    )
    slot_index = jnp.arange(P_SIZE, dtype=jnp.int32)
    valid_rows = slot_index < counts[0, 0, 0]
    own_bias = jnp.where(valid_rows, log_weight[0, 0, 0], jnp.asarray(masked_bias, jnp.bfloat16))
    face_flags = pattern[0, 0, 0] == 1
    wide_pairs, wide_bias = (
        padded(key_value[None, None, None], (("gx", 0), ("gy", 1), ("gz", 2)), 1),
        padded(own_bias[None, None, None], (("gx", 0), ("gy", 1), ("gz", 2)), 1),
    )
    face_pairs = take_faces(wide_pairs)
    face_bias = take_faces(wide_bias)
    nearby_bias = jnp.where(face_flags[:, None], face_bias.astype(jnp.float32), masked_bias)
    baffle = broadcast(baffle_store[0], ("gx", "gy", "gz"), owner_device[0])
    all_keys = jnp.concatenate([key_value, face_pairs.reshape(6 * P_SIZE, 2 * D), baffle], axis=0)
    key_bias = jnp.concatenate(
        [
            own_bias.astype(jnp.float32),
            nearby_bias.reshape(6 * P_SIZE),
            jnp.zeros((NB,), jnp.float32),
        ]
    )
    attn, log_totals = attend_forward(queries, all_keys, key_bias)
    projected = jnp.dot(attn, output_weight, preferred_element_type=jnp.float32)
    update = jnp.where(valid_rows[:, None], projected, 0.0).astype(jnp.bfloat16)
    grad_in = jnp.where(valid_rows[:, None], cotangent[0, 0, 0], jnp.zeros((), jnp.bfloat16))
    grad_attn = contract_last(grad_in, output_weight).astype(jnp.bfloat16)
    grad_q, row_dots, baffle_grad = query_back(
        queries, all_keys, key_bias, log_totals, attn, grad_attn
    )
    wide_query, wide_grad = (
        padded(queries[None, None, None], (("gx", 0), ("gy", 1), ("gz", 2)), 1),
        padded(grad_attn[None, None, None], (("gx", 0), ("gy", 1), ("gz", 2)), 1),
    )
    wide_total, wide_dots = (
        padded(log_totals[None, None, None], (("gx", 0), ("gy", 1), ("gz", 2)), 1),
        padded(row_dots[None, None, None], (("gx", 0), ("gy", 1), ("gz", 2)), 1),
    )
    query_rows = jnp.concatenate([queries[None], take_faces(wide_query)], axis=0).reshape(
        7 * P_SIZE, D
    )
    grad_rows = jnp.concatenate([grad_attn[None], take_faces(wide_grad)], axis=0).reshape(
        7 * P_SIZE, D
    )
    total_rows = jnp.transpose(
        jnp.concatenate([log_totals[None], take_faces(wide_total)], axis=0), (1, 0, 2)
    ).reshape(H, 7 * P_SIZE)
    dot_rows = jnp.transpose(
        jnp.concatenate([row_dots[None], take_faces(wide_dots)], axis=0), (1, 0, 2)
    ).reshape(H, 7 * P_SIZE)
    keep_rows = jnp.repeat(jnp.concatenate([jnp.ones((1,), bool), face_flags]), P_SIZE)
    grad_pair = key_back(
        query_rows,
        grad_rows,
        total_rows,
        dot_rows,
        keep_rows,
        key_value,
        own_bias.astype(jnp.float32),
    )
    grad_normed = contract_last(grad_q, query_weight) + contract_last(grad_pair, key_value_weight)
    grad_rows_in = layer_norm_back(grad_normed, normed, inv_std).astype(jnp.bfloat16)
    partial_terms = (
        contract_first(normed_low, grad_q).reshape(-1),
        contract_first(normed_low, grad_pair).reshape(-1),
        contract_first(attn, grad_in).reshape(-1),
        baffle_grad.reshape(-1),
    )
    totals = (
        lax.psum_scatter(partial_terms[0], ("gx", "gy", "gz"), scatter_dimension=0, tiled=True),
        lax.psum_scatter(partial_terms[1], ("gx", "gy", "gz"), scatter_dimension=0, tiled=True),
        lax.psum_scatter(partial_terms[2], ("gx", "gy", "gz"), scatter_dimension=0, tiled=True),
        lax.psum_scatter(partial_terms[3], ("gx", "gy", "gz"), scatter_dimension=0, tiled=True),
    )
    return (
        update[None, None, None],
        grad_rows_in[None, None, None],
        totals[0],
        totals[1],
        totals[2],
        totals[3],
    )


def solution(mesh):
    return jax.shard_map(
        body,
        mesh=mesh,
        in_specs=(
            P("gx", "gy", "gz", None, None),
            P("gx", "gy", "gz", None),
            P("gx", "gy", "gz"),
            P("gx", "gy", "gz", None),
            P(),
            P(),
            P(),
            P(("gx", "gy", "gz"), None, None),
            P(),
            P("gx", "gy", "gz", None, None),
        ),
        out_specs=(
            P("gx", "gy", "gz", None, None),
            P("gx", "gy", "gz", None, None),
            P(("gx", "gy", "gz")),
            P(("gx", "gy", "gz")),
            P(("gx", "gy", "gz")),
            P(("gx", "gy", "gz")),
        ),
        check_vma=False,
    )
```

profile of v0, /device:TPU:0, one launch (start us, length us, event | category | flops | bytes accessed | tf_op | source)
XLA Modules:
  0.0 870.1 jit_solution(11370236120869586524)
XLA Ops:
  15.4 5.1 collective-permute-start.6
  27.1 4.3 collective-permute-start.24
  36.1 4.7 collective-permute-start.2
  42.2 4.5 collective-permute-start.8
  49.1 5.4 collective-permute-start.26
  54.5 27.8 %collective-permute-done.8 = bf16[3,1,1,256]{3,2,1,0:T(2,128)(2,1)S(1)} collective-permute-done((bf16[3,1,1,256]{3,2,1,0:T(2,128)(2,1)S(1)}, bf16[3,1,1,256]{3,2,1,0:T(2,128)(2,1)S(1)}, u32[]{:S(2)}, u32[]{:S(2)}) %collective-permute-start.8) | collective-permute-done | bytes 1568 | tf_op jit(solution)/shard_map/ppermute | solution.py:23
  83.6 3.7 collective-permute-done.9
  88.6 4.2 collective-permute-done.11
  95.2 5.0 collective-permute-done.26
  104.2 3.7 collective-permute-start.10
  107.9 2.8 pad_maximum_fusion.3
  110.7 2.7 collective-permute-start.28
  113.4 3.8 pad_maximum_fusion.1
  117.2 3.5 collective-permute-start.4
  123.3 4.3 collective-permute-start.14
  134.6 14.6 %collective-permute-done.14 = bf16[3,1,1,256,512]{4,3,2,1,0:T(8,128)(2,1)S(1)} collective-permute-done((bf16[3,1,1,256,512]{4,3,2,1,0:T(8,128)(2,1)S(1)}, bf16[3,1,1,256,512]{4,3,2,1,0:T(8,128)(2,1)S(1)}, u32[]{:S(2)}, u32[]{:S(2)}) %collective-permute-start.14) | collective-permute-done | bytes 786464 | tf_op jit(solution)/shard_map/ppermute | solution.py:23
  150.5 4.5 collective-permute-done.15
  156.3 10.0 %collective-permute-start.16 = (bf16[3,3,1,256,512]{4,3,2,1,0:T(8,128)(2,1)S(1)}, bf16[3,3,1,256,512]{4,3,2,1,0:T(8,128)(2,1)S(1)}, u32[]{:S(2)}, u32[]{:S(2)}) collective-permute-start(bf16[3,3,1,256,512]{4,3,2,1,0:T(8,128)(2,1)S(1)} %pad_maximum_fusion.2), channel_id=1, source_target_pairs={{0,1},{2,3},{4,5},{6,7},{8,9},{10,11},{12,13},{14,15},{16,17},{18,... | collective-permute-start | bytes 7077896 | tf_op jit(solution)/shard_map/ppermute | solution.py:23
  180.8 100.8 %collective-permute-done.29 = bf16[3,3,1,256,512]{4,3,2,1,0:T(8,128)(2,1)S(1)} collective-permute-done((bf16[3,3,1,256,512]{4,3,2,1,0:T(8,128)(2,1)}, bf16[3,3,1,256,512]{4,3,2,1,0:T(8,128)(2,1)S(1)}, u32[]{:S(2)}, u32[]{:S(2)}) %collective-permute-start.29) | collective-permute-done | bytes 2359328 | tf_op jit(solution)/shard_map/ppermute | solution.py:26
  282.3 37.8 %collective-permute-done.16 = bf16[3,3,1,256,512]{4,3,2,1,0:T(8,128)(2,1)S(1)} collective-permute-done((bf16[3,3,1,256,512]{4,3,2,1,0:T(8,128)(2,1)S(1)}, bf16[3,3,1,256,512]{4,3,2,1,0:T(8,128)(2,1)S(1)}, u32[]{:S(2)}, u32[]{:S(2)}) %collective-permute-start.16) | collective-permute-done | bytes 2359328 | tf_op jit(solution)/shard_map/ppermute | solution.py:23
  320.8 11.4 %collective-permute-done.17 = bf16[3,3,1,256,512]{4,3,2,1,0:T(8,128)(2,1)S(1)} collective-permute-done((bf16[3,3,1,256,512]{4,3,2,1,0:T(8,128)(2,1)S(1)}, bf16[3,3,1,256,512]{4,3,2,1,0:T(8,128)(2,1)S(1)}, u32[]{:S(2)}, u32[]{:S(2)}) %collective-permute-start.17) | collective-permute-done | bytes 2359328 | tf_op jit(solution)/shard_map/ppermute | solution.py:26
  336.7 5.7 pad_maximum_fusion
  342.4 66.2 %while.47 = (s32[]{:T(128)}, bf16[8,256,64]{1,2,0:T(8,128)(2,1)S(1)}, f32[8,256]{1,0:T(8,128)S(1)}, s32[8]{0:T(128)S(1)}, bf16[256,512]{1,0:T(8,128)(2,1)S(1)}, ...) while((s32[]{:T(128)}, ...), condition=%wide.region_6.7_spmd, body=%wide.region_3.6_spmd.sunk | while | flops 189595392 | bytes 21780252 | solution.py:90
  347.6 3.0 fusion.149
  355.9 3.0 fusion.149
  364.2 3.0 fusion.149
  372.5 3.0 fusion.149
  380.7 3.0 fusion.149
  389.0 3.0 fusion.149
  397.3 3.0 fusion.149
  405.6 3.0 fusion.149
  408.6 121.3 %while.48 = (s32[]{:T(128)}, bf16[8,256,64]{1,2,0:T(8,128)(2,1)S(1)}, f32[8,256]{1,0:T(8,128)S(1)}, f32[8,1024,64]{1,2,0:T(8,128)}, f32[8,1024,64]{1,2,0:T(8,128...) while((s32[]{:T(128)}, ...), condition=%wide.region_9.10_spmd, body=%wide.region_7.9_spmd.sunk | while | flops 348405504 | bytes 12931952 | solution.py:117
  411.8 3.5 fusion.159
  427.0 3.5 fusion.159
  430.8 2.7 fusion.160
  442.1 3.5 fusion.159
  446.0 2.7 fusion.160
  457.3 3.5 fusion.159
  472.5 3.5 fusion.159
  476.3 2.7 fusion.160
  487.6 3.5 fusion.159
  491.5 2.7 fusion.160
  502.8 3.5 fusion.159
  506.6 2.7 fusion.160
  518.0 3.5 fusion.159
  521.8 2.7 fusion.160
  533.8 3.3 collective-permute-start.18
  538.4 2.9 copy.21
  541.4 2.9 copy.22
  547.9 3.0 copy.27
  553.4 4.2 collective-permute-start.32
  559.0 4.5 collective-permute-start.20
  569.2 3.0 collective-permute-start.22
  574.8 4.3 collective-permute-done.23
  581.1 90.0 %while.49 = (s32[]{:T(128)}, bf16[8,256,64]{1,2,0:T(8,128)(2,1)}, bf16[8,256,64]{1,2,0:T(8,128)(2,1)}, s32[8]{0:T(128)}, bf16[1792,512]{1,0:T(8,128)(2,1)}, /*in...) while((s32[]{:T(128)}, bf16[8,256,64]{1,2,0:T(8,128)(2,1)}, ...), condition=%wide.region_11.12_spmd.clone, body=%wide.region_10.11_spmd.clone.sunk | while | flops 238567424 | bytes 7658579 | solution.py:143
  589.6 2.8 fusion.172
  600.8 2.8 fusion.172
  612.1 2.8 fusion.172
  623.3 2.8 fusion.172
  634.5 2.8 fusion.172
  645.8 2.8 fusion.172
  657.1 2.8 fusion.172
  668.3 2.8 fusion.172
  679.7 177.8 %all-reduce.10.cloned.1.call-done = (f32[262144]{0:T(1024)}, f32[524288]{0:T(1024)}, f32[262144]{0:T(1024)}, f32[1048576]{0:T(1024)}) async-done(((f32[262144]{0:T(1024)}, f32[524288]{0:T(1024)}, f32[262144]{0:T(1024)}, f32[1048576]{0:T(1024)}), (f32[262144]{0:T(1024)}, f32[524288]{0:T(1024)}, f32[262144]{0:T(1024)}, f32[1048576]{0:T(1024)})) %all-reduce.10.cloned.1.call-update) | async-done | bytes 8388624
  (364 shorter events, 239.7 us)
Async XLA Ops:
  7.2 2.4 copy-start
  7.2 8.2 copy-start.16
  7.2 329.5 %all-reduce.8.cloned.1.call-start = ((), (), s32[]{:S(2)}) async-start(), calls=%async_computation | async-start | bytes 4194304 | tf_op jit(solution)/shard_map/psum | solution.py:33
  11.0 22.5 %collective-permute-start = (bf16[1,1,1,256,1024]{4,3,2,1,0:T(8,128)(2,1)S(1)}, bf16[1,1,1,256,1024]{4,3,2,1,0:T(8,128)(2,1)S(1)}, u32[]{:S(2)}, u32[]{:S(2)}) collective-permute-start(bf16[1,1,1,256,1024]{4,3,2,1,0:T(8,128)(2,1)S(1)} %bitcast.286), channel_id=1, source_target_pairs={{0,8},{8,16},{16,24},{1,9},{9,17},{17,25},{2,10},{10,18},{18,26},{... | collective-permute-start | bytes 1572872 | tf_op jit(solution)/shard_map/ppermute | solution.py:23
  13.4 21.3 %collective-permute-start.1 = (bf16[1,1,1,256,1024]{4,3,2,1,0:T(8,128)(2,1)S(1)}, bf16[1,1,1,256,1024]{4,3,2,1,0:T(8,128)(2,1)S(1)}, u32[]{:S(2)}, u32[]{:S(2)}) collective-permute-start(bf16[1,1,1,256,1024]{4,3,2,1,0:T(8,128)(2,1)S(1)} %bitcast.287), channel_id=1, source_target_pairs={{8,0},{16,8},{24,16},{9,1},{17,9},{25,17},{10,2},{18,10},{26,18},{... | collective-permute-start | bytes 1572872 | tf_op jit(solution)/shard_map/ppermute | solution.py:26
  15.4 25.4 %collective-permute-start.6 = (bf16[1,1,1,256]{3,2,1,0:T(2,128)(2,1)S(1)}, bf16[1,1,1,256]{3,2,1,0:T(2,128)(2,1)S(1)}, u32[]{:S(2)}, u32[]{:S(2)}) collective-permute-start(bf16[1,1,1,256]{3,2,1,0:T(2,128)(2,1)S(1)} %get-tuple-element.514), channel_id=1, source_target_pairs={{0,8},{8,16},{16,24},{1,9},{9,17},{17,25},{2,10},{10,18},{18,26},{... | collective-permute-start | bytes 1544 | tf_op jit(solution)/shard_map/ppermute | solution.py:23
  20.5 21.6 %collective-permute-start.7 = (bf16[1,1,1,256]{3,2,1,0:T(2,128)(2,1)S(1)}, bf16[1,1,1,256]{3,2,1,0:T(2,128)(2,1)S(1)}, u32[]{:S(2)}, u32[]{:S(2)}) collective-permute-start(bf16[1,1,1,256]{3,2,1,0:T(2,128)(2,1)S(1)} %get-tuple-element.514), channel_id=1, source_target_pairs={{8,0},{16,8},{24,16},{9,1},{17,9},{25,17},{10,2},{18,10},{26,18},{... | collective-permute-start | bytes 1544 | tf_op jit(solution)/shard_map/ppermute | solution.py:26
  24.0 7.3 copy-start.2
  24.1 833.4 %all-reduce.10.cloned.1.call-start = ((), (), s32[]{:S(2)}) async-start(), calls=%async_computation.1 | async-start | bytes 16777216
  25.0 11.2 %copy-start.17 = (pred[256]{0:T(512)(128)(4,1)}, pred[256]{0:T(512)(128)(4,1)S(1)}, u32[]{:S(2)}) copy-start(pred[256]{0:T(512)(128)(4,1)S(1)} %iota_compare_fusion) | copy-start | bytes 772
  27.1 19.7 %collective-permute-start.24 = (bf16[1,1,1,256,512]{4,3,2,1,0:T(8,128)(2,1)S(1)}, bf16[1,1,1,256,512]{4,3,2,1,0:T(8,128)(2,1)S(1)}, u32[]{:S(2)}, u32[]{:S(2)}) collective-permute-start(bf16[1,1,1,256,512]{4,3,2,1,0:T(8,128)(2,1)S(1)} %bitcast.290), channel_id=1, source_target_pairs={{0,8},{8,16},{16,24},{1,9},{9,17},{17,25},{2,10},{10,18},{18,26},{... | collective-permute-start | bytes 786440 | tf_op jit(solution)/shard_map/ppermute | solution.py:23
  31.4 90.7 %copy-start.15 = (f32[256]{0:T(256)}, f32[256]{0:T(256)S(1)}, u32[]{:S(2)}) copy-start(f32[256]{0:T(256)S(1)} %select_convert_fusion) | copy-start | bytes 3076
  31.4 10.8 %copy-start.21 = (s32[1,1,1,6]{3,2,1,0:T(1,128)S(1)}, s32[1,1,1,6]{3,2,1,0:T(1,128)}, u32[]{:S(2)}) copy-start(s32[1,1,1,6]{3,2,1,0:T(1,128)} %param.19) | copy-start | bytes 76
  33.5 14.6 %collective-permute-start.25 = (bf16[1,1,1,256,512]{4,3,2,1,0:T(8,128)(2,1)S(1)}, bf16[1,1,1,256,512]{4,3,2,1,0:T(8,128)(2,1)S(1)}, u32[]{:S(2)}, u32[]{:S(2)}) collective-permute-start(bf16[1,1,1,256,512]{4,3,2,1,0:T(8,128)(2,1)S(1)} %bitcast.291), channel_id=1, source_target_pairs={{8,0},{16,8},{24,16},{9,1},{17,9},{25,17},{10,2},{18,10},{26,18},{... | collective-permute-start | bytes 786440 | tf_op jit(solution)/shard_map/ppermute | solution.py:26
  36.1 74.5 %collective-permute-start.2 = (bf16[3,1,1,256,1024]{4,3,2,1,0:T(8,128)(2,1)}, bf16[3,1,1,256,1024]{4,3,2,1,0:T(8,128)(2,1)}, u32[]{:S(2)}, u32[]{:S(2)}) collective-permute-start(bf16[3,1,1,256,1024]{4,3,2,1,0:T(8,128)(2,1)} %pad_maximum_fusion.4), channel_id=1, source_target_pairs={{0,2},{2,4},{4,6},{1,3},{3,5},{5,7},{8,10},{10,12},{12,14},{9,11},... | collective-permute-start | bytes 4718600 | tf_op jit(solution)/shard_map/ppermute | solution.py:23
  40.8 72.6 %collective-permute-start.3 = (bf16[3,1,1,256,1024]{4,3,2,1,0:T(8,128)(2,1)}, bf16[3,1,1,256,1024]{4,3,2,1,0:T(8,128)(2,1)}, u32[]{:S(2)}, u32[]{:S(2)}) collective-permute-start(bf16[3,1,1,256,1024]{4,3,2,1,0:T(8,128)(2,1)} %pad_maximum_fusion.4), channel_id=1, source_target_pairs={{2,0},{4,2},{6,4},{3,1},{5,3},{7,5},{10,8},{12,10},{14,12},{11,9},... | collective-permute-start | bytes 4718600 | tf_op jit(solution)/shard_map/ppermute | solution.py:26
  42.2 40.1 %collective-permute-start.8 = (bf16[3,1,1,256]{3,2,1,0:T(2,128)(2,1)S(1)}, bf16[3,1,1,256]{3,2,1,0:T(2,128)(2,1)S(1)}, u32[]{:S(2)}, u32[]{:S(2)}) collective-permute-start(bf16[3,1,1,256]{3,2,1,0:T(2,128)(2,1)S(1)} %pad_maximum_fusion.16), channel_id=1, source_target_pairs={{0,2},{2,4},{4,6},{1,3},{3,5},{5,7},{8,10},{10,12},{12,14},{9,11},... | collective-permute-start | bytes 4616 | tf_op jit(solution)/shard_map/ppermute | solution.py:23
  46.7 1.3 copy-start.4
  46.8 40.5 %collective-permute-start.9 = (bf16[3,1,1,256]{3,2,1,0:T(2,128)(2,1)S(1)}, bf16[3,1,1,256]{3,2,1,0:T(2,128)(2,1)S(1)}, u32[]{:S(2)}, u32[]{:S(2)}) collective-permute-start(bf16[3,1,1,256]{3,2,1,0:T(2,128)(2,1)S(1)} %pad_maximum_fusion.16), channel_id=1, source_target_pairs={{2,0},{4,2},{6,4},{3,1},{5,3},{7,5},{10,8},{12,10},{14,12},{11,9},... | collective-permute-start | bytes 4616 | tf_op jit(solution)/shard_map/ppermute | solution.py:26
  48.1 1.0 copy-start.5
  49.1 51.2 %collective-permute-start.26 = (bf16[3,1,1,256,512]{4,3,2,1,0:T(8,128)(2,1)}, bf16[3,1,1,256,512]{4,3,2,1,0:T(8,128)(2,1)}, u32[]{:S(2)}, u32[]{:S(2)}) collective-permute-start(bf16[3,1,1,256,512]{4,3,2,1,0:T(8,128)(2,1)} %pad_maximum_fusion.6), channel_id=1, source_target_pairs={{0,2},{2,4},{4,6},{1,3},{3,5},{5,7},{8,10},{10,12},{12,14},{9,11},... | collective-permute-start | bytes 2359304 | tf_op jit(solution)/shard_map/ppermute | solution.py:23
  82.3 22.0 %collective-permute-start.27 = (bf16[3,1,1,256,512]{4,3,2,1,0:T(8,128)(2,1)}, bf16[3,1,1,256,512]{4,3,2,1,0:T(8,128)(2,1)}, u32[]{:S(2)}, u32[]{:S(2)}) collective-permute-start(bf16[3,1,1,256,512]{4,3,2,1,0:T(8,128)(2,1)} %pad_maximum_fusion.6), channel_id=1, source_target_pairs={{2,0},{4,2},{6,4},{3,1},{5,3},{7,5},{10,8},{12,10},{14,12},{11,9},... | collective-permute-start | bytes 2359304 | tf_op jit(solution)/shard_map/ppermute | solution.py:26
  87.3 5.6 collective-permute-start.11
  92.9 29.2 %collective-permute-start.12 = (bf16[1,1,1,256,512]{4,3,2,1,0:T(8,128)(2,1)S(1)}, bf16[1,1,1,256,512]{4,3,2,1,0:T(8,128)(2,1)}, u32[]{:S(2)}, u32[]{:S(2)}) collective-permute-start(bf16[1,1,1,256,512]{4,3,2,1,0:T(8,128)(2,1)S(1)} %bitcast.295), channel_id=1, source_target_pairs={{0,8},{8,16},{16,24},{1,9},{9,17},{17,25},{2,10},{10,18},{18,26},{... | collective-permute-start | bytes 786440 | tf_op jit(solution)/shard_map/ppermute | solution.py:23
  100.2 21.9 %collective-permute-start.13 = (bf16[1,1,1,256,512]{4,3,2,1,0:T(8,128)(2,1)S(1)}, bf16[1,1,1,256,512]{4,3,2,1,0:T(8,128)(2,1)}, u32[]{:S(2)}, u32[]{:S(2)}) collective-permute-start(bf16[1,1,1,256,512]{4,3,2,1,0:T(8,128)(2,1)S(1)} %bitcast.296), channel_id=1, source_target_pairs={{8,0},{16,8},{24,16},{9,1},{17,9},{25,17},{10,2},{18,10},{26,18},{... | collective-permute-start | bytes 786440 | tf_op jit(solution)/shard_map/ppermute | solution.py:26
  104.2 16.5 %collective-permute-start.10 = (bf16[3,3,1,256]{3,2,1,0:T(2,128)(2,1)S(1)}, bf16[3,3,1,256]{3,2,1,0:T(2,128)(2,1)S(1)}, u32[]{:S(2)}, u32[]{:S(2)}) collective-permute-start(bf16[3,3,1,256]{3,2,1,0:T(2,128)(2,1)S(1)} %pad_maximum_fusion.15), channel_id=1, source_target_pairs={{0,1},{2,3},{4,5},{6,7},{8,9},{10,11},{12,13},{14,15},{16,17},{18,... | collective-permute-start | bytes 13832 | tf_op jit(solution)/shard_map/ppermute | solution.py:23
  110.7 57.8 %collective-permute-start.28 = (bf16[3,3,1,256,512]{4,3,2,1,0:T(8,128)(2,1)}, bf16[3,3,1,256,512]{4,3,2,1,0:T(8,128)(2,1)}, u32[]{:S(2)}, u32[]{:S(2)}) collective-permute-start(bf16[3,3,1,256,512]{4,3,2,1,0:T(8,128)(2,1)} %pad_maximum_fusion.3), channel_id=1, source_target_pairs={{0,1},{2,3},{4,5},{6,7},{8,9},{10,11},{12,13},{14,15},{16,17},{18,... | collective-permute-start | bytes 7077896 | tf_op jit(solution)/shard_map/ppermute | solution.py:23
  117.2 215.7 %collective-permute-start.4 = (bf16[3,3,1,256,1024]{4,3,2,1,0:T(8,128)(2,1)}, bf16[3,3,1,256,1024]{4,3,2,1,0:T(8,128)(2,1)}, u32[]{:S(2)}, u32[]{:S(2)}) collective-permute-start(bf16[3,3,1,256,1024]{4,3,2,1,0:T(8,128)(2,1)} %pad_maximum_fusion.1), channel_id=1, source_target_pairs={{0,1},{2,3},{4,5},{6,7},{8,9},{10,11},{12,13},{14,15},{16,17},{18,... | collective-permute-start | bytes 14155784 | tf_op jit(solution)/shard_map/ppermute | solution.py:23
  120.7 214.1 %collective-permute-start.5 = (bf16[3,3,1,256,1024]{4,3,2,1,0:T(8,128)(2,1)}, bf16[3,3,1,256,1024]{4,3,2,1,0:T(8,128)(2,1)}, u32[]{:S(2)}, u32[]{:S(2)}) collective-permute-start(bf16[3,3,1,256,1024]{4,3,2,1,0:T(8,128)(2,1)} %pad_maximum_fusion.1), channel_id=1, source_target_pairs={{1,0},{3,2},{5,4},{7,6},{9,8},{11,10},{13,12},{15,14},{17,16},{19,... | collective-permute-start | bytes 14155784 | tf_op jit(solution)/shard_map/ppermute | solution.py:26
  122.1 8.4 copy-start.6
  123.3 25.9 %collective-permute-start.14 = (bf16[3,1,1,256,512]{4,3,2,1,0:T(8,128)(2,1)S(1)}, bf16[3,1,1,256,512]{4,3,2,1,0:T(8,128)(2,1)S(1)}, u32[]{:S(2)}, u32[]{:S(2)}) collective-permute-start(bf16[3,1,1,256,512]{4,3,2,1,0:T(8,128)(2,1)S(1)} %pad_maximum_fusion.5), channel_id=1, source_target_pairs={{0,2},{2,4},{4,6},{1,3},{3,5},{5,7},{8,10},{10,12},{12,14},{9,11},... | collective-permute-start | bytes 2359304 | tf_op jit(solution)/shard_map/ppermute | solution.py:23
  127.6 27.4 %collective-permute-start.15 = (bf16[3,1,1,256,512]{4,3,2,1,0:T(8,128)(2,1)S(1)}, bf16[3,1,1,256,512]{4,3,2,1,0:T(8,128)(2,1)S(1)}, u32[]{:S(2)}, u32[]{:S(2)}) collective-permute-start(bf16[3,1,1,256,512]{4,3,2,1,0:T(8,128)(2,1)S(1)} %pad_maximum_fusion.5), channel_id=1, source_target_pairs={{2,0},{4,2},{6,4},{3,1},{5,3},{7,5},{10,8},{12,10},{14,12},{11,9},... | collective-permute-start | bytes 2359304 | tf_op jit(solution)/shard_map/ppermute | solution.py:26
  149.2 132.4 %collective-permute-start.29 = (bf16[3,3,1,256,512]{4,3,2,1,0:T(8,128)(2,1)}, bf16[3,3,1,256,512]{4,3,2,1,0:T(8,128)(2,1)S(1)}, u32[]{:S(2)}, u32[]{:S(2)}) collective-permute-start(bf16[3,3,1,256,512]{4,3,2,1,0:T(8,128)(2,1)} %pad_maximum_fusion.3), channel_id=1, source_target_pairs={{1,0},{3,2},{5,4},{7,6},{9,8},{11,10},{13,12},{15,14},{17,16},{19,... | collective-permute-start | bytes 7077896 | tf_op jit(solution)/shard_map/ppermute | solution.py:26
  156.3 163.8 %collective-permute-start.16 = (bf16[3,3,1,256,512]{4,3,2,1,0:T(8,128)(2,1)S(1)}, bf16[3,3,1,256,512]{4,3,2,1,0:T(8,128)(2,1)S(1)}, u32[]{:S(2)}, u32[]{:S(2)}) collective-permute-start(bf16[3,3,1,256,512]{4,3,2,1,0:T(8,128)(2,1)S(1)} %pad_maximum_fusion.2), channel_id=1, source_target_pairs={{0,1},{2,3},{4,5},{6,7},{8,9},{10,11},{12,13},{14,15},{16,17},{18,... | collective-permute-start | bytes 7077896 | tf_op jit(solution)/shard_map/ppermute | solution.py:23
  168.5 163.7 %collective-permute-start.17 = (bf16[3,3,1,256,512]{4,3,2,1,0:T(8,128)(2,1)S(1)}, bf16[3,3,1,256,512]{4,3,2,1,0:T(8,128)(2,1)S(1)}, u32[]{:S(2)}, u32[]{:S(2)}) collective-permute-start(bf16[3,3,1,256,512]{4,3,2,1,0:T(8,128)(2,1)S(1)} %pad_maximum_fusion.2), channel_id=1, source_target_pairs={{1,0},{3,2},{5,4},{7,6},{9,8},{11,10},{13,12},{15,14},{17,16},{19,... | collective-permute-start | bytes 7077896 | tf_op jit(solution)/shard_map/ppermute | solution.py:26
  345.5 1.6 copy-start.1
  353.7 1.6 copy-start.1
  362.0 1.6 copy-start.1
  370.3 1.6 copy-start.1
  378.6 1.6 copy-start.1
  386.8 1.6 copy-start.1
  395.1 1.6 copy-start.1
  403.4 1.6 copy-start.1
  529.9 14.4 %copy-start.7 = (bf16[8,256,64]{1,2,0:T(8,128)(2,1)}, bf16[8,256,64]{1,2,0:T(8,128)(2,1)S(1)}, u32[]{:S(2)}) copy-start(bf16[8,256,64]{1,2,0:T(8,128)(2,1)S(1)} %get-tuple-element.388) | copy-start | bytes 786436
  529.9 17.6 %copy-start.9 = (bf16[256,512]{0,1:T(8,128)(2,1)}, bf16[256,512]{0,1:T(8,128)(2,1)S(1)}, u32[]{:S(2)}) copy-start(bf16[256,512]{0,1:T(8,128)(2,1)S(1)} %get-tuple-element.894) | copy-start | bytes 786436
  529.9 23.5 %collective-permute-start.30 = (f32[1,1,1,8,256]{4,3,2,1,0:T(8,128)S(1)}, f32[1,1,1,8,256]{4,3,2,1,0:T(8,128)S(1)}, u32[]{:S(2)}, u32[]{:S(2)}) collective-permute-start(f32[1,1,1,8,256]{4,3,2,1,0:T(8,128)S(1)} %bitcast.314), channel_id=1, source_target_pairs={{0,8},{8,16},{16,24},{1,9},{9,17},{17,25},{2,10},{10,18},{18,26},{... | collective-permute-start | bytes 24584 | tf_op jit(solution)/shard_map/ppermute | solution.py:23
  532.4 21.0 %collective-permute-start.31 = (f32[1,1,1,8,256]{4,3,2,1,0:T(8,128)S(1)}, f32[1,1,1,8,256]{4,3,2,1,0:T(8,128)S(1)}, u32[]{:S(2)}, u32[]{:S(2)}) collective-permute-start(f32[1,1,1,8,256]{4,3,2,1,0:T(8,128)S(1)} %bitcast.315), channel_id=1, source_target_pairs={{8,0},{16,8},{24,16},{9,1},{17,9},{25,17},{10,2},{18,10},{26,18},{... | collective-permute-start | bytes 24584 | tf_op jit(solution)/shard_map/ppermute | solution.py:26
  533.8 25.1 %collective-permute-start.18 = (f32[1,1,1,8,256]{4,3,2,1,0:T(8,128)S(1)}, f32[1,1,1,8,256]{4,3,2,1,0:T(8,128)S(1)}, u32[]{:S(2)}, u32[]{:S(2)}) collective-permute-start(f32[1,1,1,8,256]{4,3,2,1,0:T(8,128)S(1)} %bitcast.310), channel_id=1, source_target_pairs={{0,8},{8,16},{16,24},{1,9},{9,17},{17,25},{2,10},{10,18},{18,26},{... | collective-permute-start | bytes 24584 | tf_op jit(solution)/shard_map/ppermute | solution.py:23
  537.1 21.8 %collective-permute-start.19 = (f32[1,1,1,8,256]{4,3,2,1,0:T(8,128)S(1)}, f32[1,1,1,8,256]{4,3,2,1,0:T(8,128)S(1)}, u32[]{:S(2)}, u32[]{:S(2)}) collective-permute-start(f32[1,1,1,8,256]{4,3,2,1,0:T(8,128)S(1)} %bitcast.311), channel_id=1, source_target_pairs={{8,0},{16,8},{24,16},{9,1},{17,9},{25,17},{10,2},{18,10},{26,18},{... | collective-permute-start | bytes 24584 | tf_op jit(solution)/shard_map/ppermute | solution.py:26
  544.8 2.7 copy-start.14
  544.8 2.7 copy-start.18
  553.4 11.4 %collective-permute-start.32 = (f32[3,1,1,8,256]{4,3,2,1,0:T(8,128)S(1)}, f32[3,1,1,8,256]{4,3,2,1,0:T(8,128)S(1)}, u32[]{:S(2)}, u32[]{:S(2)}) collective-permute-start(f32[3,1,1,8,256]{4,3,2,1,0:T(8,128)S(1)} %pad_maximum_fusion.13), channel_id=1, source_target_pairs={{0,2},{2,4},{4,6},{1,3},{3,5},{5,7},{8,10},{10,12},{12,14},{9,11},... | collective-permute-start | bytes 73736 | tf_op jit(solution)/shard_map/ppermute | solution.py:23
  557.6 7.2 collective-permute-start.33
  559.0 8.7 %collective-permute-start.20 = (f32[3,1,1,8,256]{4,3,2,1,0:T(8,128)S(1)}, f32[3,1,1,8,256]{4,3,2,1,0:T(8,128)S(1)}, u32[]{:S(2)}, u32[]{:S(2)}) collective-permute-start(f32[3,1,1,8,256]{4,3,2,1,0:T(8,128)S(1)} %pad_maximum_fusion.12), channel_id=1, source_target_pairs={{0,2},{2,4},{4,6},{1,3},{3,5},{5,7},{8,10},{10,12},{12,14},{9,11},... | collective-permute-start | bytes 73736 | tf_op jit(solution)/shard_map/ppermute | solution.py:23
  563.5 5.7 collective-permute-start.21
  564.9 8.7 %collective-permute-start.34 = (f32[3,3,1,8,256]{4,3,2,1,0:T(8,128)S(1)}, f32[3,3,1,8,256]{4,3,2,1,0:T(8,128)S(1)}, u32[]{:S(2)}, u32[]{:S(2)}) collective-permute-start(f32[3,3,1,8,256]{4,3,2,1,0:T(8,128)S(1)} %pad_maximum_fusion.11), channel_id=1, source_target_pairs={{0,1},{2,3},{4,5},{6,7},{8,9},{10,11},{12,13},{14,15},{16,17},{18,... | collective-permute-start | bytes 221192 | tf_op jit(solution)/shard_map/ppermute | solution.py:23
  566.4 7.3 collective-permute-start.35
  569.2 5.6 collective-permute-start.22
  572.3 6.8 collective-permute-start.23
  674.6 1.1 copy-start.20
  674.6 2.2 copy-start.8
  674.7 2.2 copy-start.12
  674.7 2.5 copy-start.3
  674.7 2.5 copy-start.11
  (3 other events, 2.9 us)
Sparse Core Ops, SparseCore 0:
  24.2 142.4 all-reduce.7
  674.8 182.5 all-reduce.9
where the time goes:
time: 875 us; the launch traced here: 870 us
  waiting for transfers between devices  399 us (46%)
  matrix products  200 us (23%)
  starting transfers between devices  95.3 us (11%)
  local copies, waits for them, and re-layouts  81.5 us (9%)
  loops' own time  47.9 us (5%)
  other arithmetic  30.6 us (3%)
  between operations  16.2 us (2%)
    unnamed x3, waiting for transfers between devices  178 us
    ppermute x18, waiting for transfers between devices, padded(): lax.ppermute(lax.slice_in_dim(block, 0, width, axis=dim), axis, backward)  133 us
    ppermute x18, waiting for transfers between devices, padded(): lax.ppermute(lax.slice_in_dim(block, block.shape[dim] - width, None, axis...  87.8 us
    dot_general x35, matrix products, contract_last(): lax.dot_general(left, right, (((1,), (1,)), ((), ())), preferred_element_...  86.7 us
    ppermute x18, starting transfers between devices, padded(): lax.ppermute(lax.slice_in_dim(block, block.shape[dim] - width, None, axis...  71.8 us
    dot_general x35, matrix products, contract_first(): lax.dot_general(left, right, (((0,), (0,)), ((), ())), preferred_element_...  68.7 us
    unnamed x77, local copies, waits for them, and re-layouts  35.4 us
    dot_general x8, matrix products, attend_per_head(): jnp.dot(prob_low, value_head, preferred_element_type=jnp.float32)  23.7 us
  transfers between devices with their start and end apart: 38, of which 15 were waited for; matrix products, arithmetic and copies ran while one was open for 7% of the time, Pallas kernels for 0%

commit v1 on v0

v1 whole, which is shorter than its diff:
```python
import functools
import math

import jax
import jax.numpy as jnp
from jax import lax
from jax.experimental import pallas as pl
from jax.experimental.pallas import tpu as pltpu
from jax.sharding import PartitionSpec as P

D = 512
H = 8
HD = 64
P_SIZE = 256
NB = 1024
LANES = 128
PAIR = 2 * HD
AUG = 2 * D + LANES
NEAR = 7 * P_SIZE
ALL = NEAR + NB
PIECE = 32

masked_bias = -1000000000.0
F32 = jnp.float32
BF16 = jnp.bfloat16
MESH = pl.DeviceIdType.MESH
VMEM_BYTES = 56 * 1024 * 1024


def nt(left, right):
    return lax.dot_general(left, right, (((1,), (1,)), ((), ())), preferred_element_type=F32)


def tn(left, right):
    return lax.dot_general(left, right, (((0,), (0,)), ((), ())), preferred_element_type=F32)


def nn(left, right):
    return jnp.dot(left, right, preferred_element_type=F32)


def layer_norm(values):
    row_mean = jnp.mean(values, axis=-1, keepdims=True)
    centered = values - row_mean
    inv_std = lax.rsqrt(jnp.mean(centered * centered, axis=-1, keepdims=True) + 1e-05)
    return (centered * inv_std, inv_std)


class Place:
    def __init__(self, sizes):
        self.sizes = sizes
        gx, gy, gz = sizes
        self.at = (lax.axis_index("gx"), lax.axis_index("gy"), lax.axis_index("gz"))
        self.counts = {"y": gx // 2, "c": 2, "gy": gy, "gz": gz}
        self.pos = {
            "y": self.at[0] // 2,
            "c": self.at[0] % 2,
            "gy": self.at[1],
            "gz": self.at[2],
        }

    def device(self, axis, position):
        pos = dict(self.pos)
        pos[axis] = position
        return (pos["y"] * 2 + pos["c"], pos["gy"], pos["gz"])

    def barrier(self):
        sem = pltpu.get_barrier_semaphore()
        total = 0
        for dim, count in enumerate(self.sizes):
            for step in range(1, count):
                target = list(self.at)
                target[dim] = lax.rem(self.at[dim] + step, count)
                pl.semaphore_signal(sem, inc=1, device_id=tuple(target), device_id_type=MESH)
                total += 1
        pl.semaphore_wait(sem, total)

    def faces(self):
        found = []
        for dim, count in enumerate(self.sizes):
            for side in (-1, 1):
                there = self.at[dim] > 0 if side < 0 else self.at[dim] < count - 1
                target = list(self.at)
                target[dim] = jnp.clip(self.at[dim] + side, 0, count - 1)
                found.append((there, tuple(target)))
        return found


AXES = ("y", "c", "gy", "gz")
ORDERS = (("c", "gz", "y", "gy"), ("c", "y", "gz", "gy"))


def select(fixed, rows):
    return tuple(fixed.get(axis, slice(None)) for axis in AXES) + (rows, slice(None))


def stage_plan(sizes):
    gx, gy, gz = sizes
    counts = {"y": gx // 2, "c": 2, "gy": gy, "gz": gz}
    plan = []
    for half, order in enumerate(ORDERS):
        done = []
        for axis in order:
            done.append(axis)
            left = tuple(counts[a] for a in AXES if a not in done)
            plan.append((half, axis, counts[axis], left))
    return counts, plan


def scatter_scratch(sizes, width):
    counts, plan = stage_plan(sizes)
    rows = PIECE // 2
    shapes = [pltpu.VMEM((n - 1,) + left + (rows, width), BF16) for _, _, n, left in plan]
    copies = sum(n - 1 for _, _, n, _ in plan)
    work = pltpu.VMEM((counts["y"], 2, counts["gy"], counts["gz"], PIECE, width), BF16)
    return shapes + [work, pltpu.SemaphoreType.DMA((copies,)), pltpu.SemaphoreType.DMA((copies,))]


class Scatter:
    def __init__(self, place, source, scratch):
        self.place = place
        self.source = source
        self.recv = scratch[:8]
        self.work, self.send_sem, self.recv_sem = scratch[8:11]
        self.plan = stage_plan(place.sizes)[1]
        self.offsets = []
        total = 0
        for _, _, n, _ in self.plan:
            self.offsets.append(total)
            total += n - 1

    def rows(self, half):
        return pl.ds(half * (PIECE // 2), PIECE // 2)

    def fixed(self, half, level):
        return {axis: self.place.pos[axis] for axis in ORDERS[half][:level]}

    def copies(self, half, level):
        at = half * 4 + level
        axis, n = self.plan[at][1], self.plan[at][2]
        origin = self.source if level == 0 else self.work
        found = []
        for step in range(1, n):
            target = lax.rem(self.place.pos[axis] + step, n)
            fixed = self.fixed(half, level)
            fixed[axis] = target
            found.append(
                pltpu.make_async_remote_copy(
                    src_ref=origin.at[select(fixed, self.rows(half))],
                    dst_ref=self.recv[at].at[step - 1],
                    send_sem=self.send_sem.at[self.offsets[at] + step - 1],
                    recv_sem=self.recv_sem.at[self.offsets[at] + step - 1],
                    device_id=self.place.device(axis, target),
                    device_id_type=MESH,
                )
            )
        return found

    def start(self, level):
        for half in range(2):
            for copy in self.copies(half, level):
                copy.start()

    def finish(self, level, out=None):
        for half in range(2):
            at = half * 4 + level
            for copy in self.copies(half, level):
                copy.wait()
            origin = self.source if level == 0 else self.work
            where = select(self.fixed(half, level + 1), self.rows(half))
            total = origin[where].astype(F32)
            for step in range(self.plan[at][2] - 1):
                total = total + self.recv[at][step].astype(F32)
            if out is None:
                self.work[where] = total.astype(BF16)
            else:
                out[self.rows(half), :] = total.astype(out.dtype)


def gather_copies(place, final, send_sem, recv_sem, level):
    counts, plan = stage_plan(place.sizes)
    found = []
    for half in range(2):
        order = ORDERS[half]
        axis = order[level]
        base = sum(n - 1 for h, a, n, _ in plan[: half * 4 + level])
        fixed = {a: place.pos[a] for a in order[: level + 1]}
        view = final.at[select(fixed, pl.ds(half * (PIECE // 2), PIECE // 2))]
        for step in range(1, counts[axis]):
            target = lax.rem(place.pos[axis] + step, counts[axis])
            found.append(
                pltpu.make_async_remote_copy(
                    src_ref=view,
                    dst_ref=view,
                    send_sem=send_sem.at[base + step - 1],
                    recv_sem=recv_sem.at[base + step - 1],
                    device_id=place.device(axis, target),
                    device_id_type=MESH,
                )
            )
    return found


def project_kernel(sizes, rows_ref, bias_ref, wq, wkv, wo, gin, baf, q_out, g_out, keys, final,
                   *scratch):
    scatter_refs, (gs, gr, hs, hr, piece) = scratch[:11], scratch[11:]
    place = Place(sizes)
    place.barrier()
    scatter = Scatter(place, baf, scatter_refs)
    scatter.start(0)
    normed_low = layer_norm(rows_ref[...].astype(F32))[0].astype(BF16)
    keys[0:P_SIZE, 0 : 2 * D] = nn(normed_low, wkv[...]).astype(BF16)
    keys[0:P_SIZE, 2 * D : AUG] = bias_ref[...]
    faces = place.faces()

    def face_copy(face, slot):
        return pltpu.make_async_remote_copy(
            src_ref=keys.at[pl.ds(0, P_SIZE)],
            dst_ref=keys.at[pl.ds((1 + slot) * P_SIZE, P_SIZE)],
            send_sem=hs.at[face],
            recv_sem=hr.at[slot],
            device_id=faces[face][1],
            device_id_type=MESH,
        )

    scatter.finish(0)
    scatter.start(1)
    for face, (there, _) in enumerate(faces):
        @pl.when(there)
        def _(face=face):
            face_copy(face, face ^ 1).start()

        @pl.when(jnp.logical_not(there))
        def _(face=face):
            keys[(1 + face) * P_SIZE : (2 + face) * P_SIZE, :] = jnp.zeros((P_SIZE, AUG), BF16)

    q_out[...] = nn(normed_low, wq[...]).astype(BF16)
    g_out[...] = nt(gin[...], wo[...]).astype(BF16)
    scatter.finish(1)
    scatter.start(2)
    scatter.finish(2)
    scatter.start(3)
    scatter.finish(3, piece)
    final[place.pos["y"], place.pos["c"], place.pos["gy"], place.pos["gz"]] = piece[...]
    for level in (3, 2, 1, 0):
        sent = gather_copies(place, final, gs, gr, level)
        for copy in sent:
            copy.start()
        for copy in sent:
            copy.wait()
    for face, (there, _) in enumerate(faces):
        @pl.when(there)
        def _(face=face):
            face_copy(face, face ^ 1).wait_send()
            face_copy(face, face).wait_recv()


def attend_kernel(flags, q_ref, g_ref, k_ref, v_ref, b_ref, bk_ref, bv_ref,
                  attn_ref, gq_ref, dk_ref, dv_ref, dbk_ref, dbv_ref, e_scr, p_scr, d_scr):
    lane = lax.broadcasted_iota(jnp.int32, (P_SIZE, PAIR), 1)
    zero = jnp.zeros((P_SIZE, PAIR), BF16)
    q = q_ref[...] * jnp.asarray(1.0 / math.sqrt(HD), BF16)
    g = g_ref[...]
    qcat = jnp.concatenate([jnp.where(lane < HD, q, zero), jnp.where(lane < HD, zero, q)], axis=0)
    gcat = jnp.concatenate([jnp.where(lane < HD, g, zero), jnp.where(lane < HD, zero, g)], axis=0)
    first = (lax.broadcasted_iota(jnp.int32, (2 * P_SIZE, LANES), 1) == 0).astype(BF16)
    qaug = jnp.concatenate([qcat, first], axis=1)
    chunks = ALL // P_SIZE

    def part(c):
        if c < 7:
            return slice(c * P_SIZE, (c + 1) * P_SIZE), k_ref, v_ref, dk_ref, dv_ref
        return slice((c - 7) * P_SIZE, (c - 6) * P_SIZE), bk_ref, bv_ref, dbk_ref, dbv_ref

    top = jnp.full((8, 2 * P_SIZE), -3e38, F32)
    for c in range(chunks):
        rows, keys = part(c)[:2]
        if c < 7:
            bias = b_ref[rows, :]
            if c > 0:
                bias = jnp.where(flags[c - 1] == 1, bias, jnp.asarray(masked_bias, BF16))
            scores = nt(jnp.concatenate([keys[rows, :], bias], axis=1), qaug)
        else:
            scores = nt(keys[rows, :], qcat)
        e_scr[c * P_SIZE : (c + 1) * P_SIZE, :] = scores
        top = jnp.maximum(top, jnp.max(scores.reshape(P_SIZE // 8, 8, 2 * P_SIZE), axis=0))
    top = jnp.max(top, axis=0, keepdims=True)
    total = jnp.zeros((8, 2 * P_SIZE), F32)
    for c in range(chunks):
        span = slice(c * P_SIZE, (c + 1) * P_SIZE)
        e = jnp.exp(e_scr[span, :] - top)
        e_scr[span, :] = e
        total = total + jnp.sum(e.reshape(P_SIZE // 8, 8, 2 * P_SIZE), axis=0)
    inverse = 1.0 / jnp.sum(total, axis=0, keepdims=True)
    attn_t = jnp.zeros((PAIR, 2 * P_SIZE), F32)
    for c in range(chunks):
        span = slice(c * P_SIZE, (c + 1) * P_SIZE)
        rows, _, values = part(c)[:3]
        p = (e_scr[span, :] * inverse).astype(BF16)
        p_scr[span, :] = p
        attn_t = attn_t + tn(values[rows, :], p)
    picked = jnp.concatenate([attn_t[:HD, :P_SIZE], attn_t[HD:, P_SIZE:]], axis=0)
    attn_ref[...] = picked.T.astype(BF16)
    product = g.astype(F32).T * picked.astype(BF16).astype(F32)
    row_dot = jnp.concatenate(
        [
            jnp.sum(product[:HD], axis=0, keepdims=True),
            jnp.sum(product[HD:], axis=0, keepdims=True),
        ],
        axis=1,
    )
    gq_t = jnp.zeros((PAIR, 2 * P_SIZE), F32)
    for c in range(chunks):
        span = slice(c * P_SIZE, (c + 1) * P_SIZE)
        rows, keys, values, dkeys, dvalues = part(c)
        grad_prob = nt(values[rows, :], gcat)
        ds = (e_scr[span, :] * inverse * (grad_prob - row_dot)).astype(BF16)
        gq_t = gq_t + tn(keys[rows, :], ds)
        dkeys[rows, :] = nn(ds, qcat).astype(BF16)
        dvalues[rows, :] = nn(p_scr[span, :], gcat).astype(BF16)
    picked_q = jnp.concatenate([gq_t[:HD, :P_SIZE], gq_t[HD:, P_SIZE:]], axis=0)
    gq_ref[...] = (picked_q.T * (1.0 / math.sqrt(HD))).astype(BF16)


def return_kernel(sizes, rows_ref, wq, wkv, gin, attn, gq, dk, dv, base,
                  grad_out, wkv_out, wqo_out, base_out, rk, rv, *scratch):
    scatter_refs, (ss, rs) = scratch[:11], scratch[11:]
    place = Place(sizes)
    place.barrier()
    faces = place.faces()

    def face_copy(face, slot, which):
        source, target = ((dk, rk), (dv, rv))[which]
        return pltpu.make_async_remote_copy(
            src_ref=source.at[pl.ds((1 + face) * P_SIZE, P_SIZE)],
            dst_ref=target.at[slot],
            send_sem=ss.at[2 * face + which],
            recv_sem=rs.at[2 * slot + which],
            device_id=faces[face][1],
            device_id_type=MESH,
        )

    for face, (there, _) in enumerate(faces):
        @pl.when(there)
        def _(face=face):
            face_copy(face, face ^ 1, 0).start()
            face_copy(face, face ^ 1, 1).start()

        @pl.when(jnp.logical_not(there))
        def _(face=face):
            rk[face] = jnp.zeros((P_SIZE, D), BF16)
            rv[face] = jnp.zeros((P_SIZE, D), BF16)

    scatter = Scatter(place, base, scatter_refs)
    scatter.start(0)
    normed, inv_std = layer_norm(rows_ref[...].astype(F32))
    normed_low = normed.astype(BF16)
    wqo_out[:, :D] = tn(normed_low, gq[...]).astype(BF16)
    wqo_out[:, D:] = tn(attn[...], gin[...]).astype(BF16)
    scatter.finish(0)
    scatter.start(1)
    for face, (there, _) in enumerate(faces):
        @pl.when(there)
        def _(face=face):
            for which in range(2):
                face_copy(face, face ^ 1, which).wait_send()
                face_copy(face, face, which).wait_recv()
    scatter.finish(1)
    scatter.start(2)
    sum_k = dk[0:P_SIZE, :].astype(F32)
    sum_v = dv[0:P_SIZE, :].astype(F32)
    for face in range(6):
        sum_k = sum_k + rk[face].astype(F32)
        sum_v = sum_v + rv[face].astype(F32)
    pair_k = sum_k.astype(BF16)
    pair_v = sum_v.astype(BF16)
    wkv_out[:, :D] = tn(normed_low, pair_k).astype(BF16)
    wkv_out[:, D:] = tn(normed_low, pair_v).astype(BF16)
    scatter.finish(2)
    scatter.start(3)
    grad = nt(gq[...], wq[...]) + nt(pair_k, wkv[:, :D]) + nt(pair_v, wkv[:, D:])
    first_mean = jnp.mean(grad, axis=-1, keepdims=True)
    second_mean = jnp.mean(grad * normed, axis=-1, keepdims=True)
    grad_out[...] = (inv_std * (grad - first_mean - normed * second_mean)).astype(BF16)
    scatter.finish(3, base_out)


def scatter_kernel(sizes, source, out, *scratch):
    place = Place(sizes)
    place.barrier()
    scatter = Scatter(place, source, scratch)
    for level in range(4):
        scatter.start(level)
        scatter.finish(level, out if level == 3 else None)


def vmem():
    return pl.BlockSpec(memory_space=pltpu.VMEM)


def shape(dims, dtype):
    return jax.ShapeDtypeStruct(dims, dtype)


def remote(kernel, sizes, outs, scratch, collective, operands):
    return pl.pallas_call(
        functools.partial(kernel, sizes),
        out_shape=outs,
        in_specs=[vmem()] * len(operands),
        out_specs=jax.tree.map(lambda _: vmem(), outs),
        scratch_shapes=scratch,
        compiler_params=pltpu.CompilerParams(
            collective_id=collective, has_side_effects=True, vmem_limit_bytes=VMEM_BYTES
        ),
    )(*operands)


def attend(flags, q, g, keys, baffle):
    def cols(rows, shift):
        return pl.BlockSpec((rows, PAIR), lambda p: (0, p + shift))

    groups = D // PAIR
    return pl.pallas_call(
        attend_kernel,
        grid=(groups,),
        out_shape=(
            shape((P_SIZE, D), BF16),
            shape((P_SIZE, D), BF16),
            shape((NEAR, D), BF16),
            shape((NEAR, D), BF16),
            shape((NB, D), BF16),
            shape((NB, D), BF16),
        ),
        in_specs=[
            pl.BlockSpec(memory_space=pltpu.SMEM),
            cols(P_SIZE, 0),
            cols(P_SIZE, 0),
            cols(NEAR, 0),
            cols(NEAR, groups),
            pl.BlockSpec((NEAR, PAIR), lambda p: (0, 2 * groups)),
            cols(NB, 0),
            cols(NB, groups),
        ],
        out_specs=(
            cols(P_SIZE, 0),
            cols(P_SIZE, 0),
            cols(NEAR, 0),
            cols(NEAR, 0),
            cols(NB, 0),
            cols(NB, 0),
        ),
        scratch_shapes=[
            pltpu.VMEM((ALL, 2 * P_SIZE), F32),
            pltpu.VMEM((ALL, 2 * P_SIZE), BF16),
            pltpu.VMEM((8, LANES), BF16),
        ],
        compiler_params=pltpu.CompilerParams(vmem_limit_bytes=VMEM_BYTES),
    )(flags, q, g, keys, keys, keys, baffle, baffle)


def body(
    sizes,
    particles,
    log_weight,
    counts,
    pattern,
    query_weight,
    key_value_weight,
    output_weight,
    baffle_store,
    owner_device,
    cotangent,
):
    gx, gy, gz = sizes
    devices = gx * gy * gz
    rows_in = particles[0, 0, 0]
    valid_rows = jnp.arange(P_SIZE, dtype=jnp.int32) < counts[0, 0, 0]
    own_bias = jnp.where(valid_rows, log_weight[0, 0, 0], jnp.asarray(masked_bias, BF16))
    bias_lanes = jnp.broadcast_to(own_bias[:, None], (P_SIZE, LANES))
    grad_in = jnp.where(valid_rows[:, None], cotangent[0, 0, 0], jnp.zeros((), BF16))
    me = lax.axis_index(("gx", "gy", "gz"))
    width = NB * 2 * D // (devices * PIECE)
    pieces = (gx // 2, 2, gy, gz, PIECE, width)
    store = jnp.where(me == owner_device[0], baffle_store[0], jnp.zeros((), BF16)).reshape(pieces)
    copies = sum(n - 1 for _, _, n, _ in stage_plan(sizes)[1])
    dma = pltpu.SemaphoreType.DMA
    q, g, keys, final = remote(
        project_kernel,
        sizes,
        (
            shape((P_SIZE, D), BF16),
            shape((P_SIZE, D), BF16),
            shape((NEAR, AUG), BF16),
            shape(pieces, BF16),
        ),
        scatter_scratch(sizes, width)
        + [dma((copies,)), dma((copies,)), dma((6,)), dma((6,)), pltpu.VMEM((PIECE, width), BF16)],
        0,
        (rows_in, bias_lanes, query_weight, key_value_weight, output_weight, grad_in, store),
    )
    baffle = final.reshape(NB, 2 * D)
    attn, gq, dk, dv, dbk, dbv = attend(pattern[0, 0, 0], q, g, keys, baffle)
    projected = nn(attn, output_weight)
    update = jnp.where(valid_rows[:, None], projected, 0.0).astype(BF16)
    base = jnp.concatenate([dbk, dbv], axis=1).reshape(pieces)
    grad_rows, w_kv, w_qo, base_sum = remote(
        return_kernel,
        sizes,
        (
            shape((P_SIZE, D), BF16),
            shape((D, 2 * D), BF16),
            shape((D, 2 * D), BF16),
            shape((PIECE, width), F32),
        ),
        [pltpu.VMEM((6, P_SIZE, D), BF16), pltpu.VMEM((6, P_SIZE, D), BF16)]
        + scatter_scratch(sizes, width)
        + [dma((12,)), dma((12,))],
        1,
        (rows_in, query_weight, key_value_weight, grad_in, attn, gq, dk, dv, base),
    )
    if width == 2 * D:
        half = PIECE // 2
        weights = jnp.concatenate(
            [w_kv.reshape(devices, half, width), w_qo.reshape(devices, half, width)], axis=1
        )
    else:
        weights = jnp.concatenate(
            [
                w_kv.reshape(devices, -1),
                w_qo[:, :D].reshape(devices, -1),
                w_qo[:, D:].reshape(devices, -1),
            ],
            axis=1,
        )
    weight_sum = remote(
        scatter_kernel,
        sizes,
        shape((PIECE, width), F32),
        scatter_scratch(sizes, width),
        2,
        (weights.reshape(pieces),),
    )
    if width == 2 * D:
        grad_kv = weight_sum[:half].reshape(-1)
        grad_q = weight_sum[half:, :D].reshape(-1)
        grad_o = weight_sum[half:, D:].reshape(-1)
    else:
        flat = weight_sum.reshape(-1)
        part = D * D // devices
        grad_kv, grad_q, grad_o = flat[: 2 * part], flat[2 * part : 3 * part], flat[3 * part :]
    return (
        update[None, None, None],
        grad_rows[None, None, None],
        grad_q,
        grad_kv,
        grad_o,
        base_sum.reshape(-1),
    )


def solution(mesh):
    sizes = tuple(mesh.shape[axis] for axis in ("gx", "gy", "gz"))
    return jax.shard_map(
        functools.partial(body, sizes),
        mesh=mesh,
        in_specs=(
            P("gx", "gy", "gz", None, None),
            P("gx", "gy", "gz", None),
            P("gx", "gy", "gz"),
            P("gx", "gy", "gz", None),
            P(),
            P(),
            P(),
            P(("gx", "gy", "gz"), None, None),
            P(),
            P("gx", "gy", "gz", None, None),
        ),
        out_specs=(
            P("gx", "gy", "gz", None, None),
            P("gx", "gy", "gz", None, None),
            P(("gx", "gy", "gz")),
            P(("gx", "gy", "gz")),
            P(("gx", "gy", "gz")),
            P(("gx", "gy", "gz")),
        ),
        check_vma=False,
    )
```

time: 875 us -> 176 us (0.20)
  waiting for transfers between devices: 399 us -> 0 us
  matrix products: 200 us -> 1.96 us
  Pallas kernels: 0 us -> 155 us
  starting transfers between devices: 95.3 us -> 0 us
  local copies, waits for them, and re-layouts: 81.5 us -> 5.65 us
  loops' own time: 47.9 us -> 0 us
  other arithmetic: 30.6 us -> 10.2 us
  between operations: 16.2 us -> 1.99 us
    ppermute x36 -> x0, waiting for transfers between devices: 221 us -> none  [the longest x18 133 us: padded(): lax.ppermute(lax.slice_in_dim(block, 0, width, axis=dim), axis, backward)]
    dot_general x89 -> x1, matrix products: 200 us -> 1.96 us  [nn(): return jnp.dot(left, right, preferred_element_type=F32)]
    unnamed x3 -> x0, waiting for transfers between devices: 178 us -> none
    pallas_call x0 -> x4, Pallas kernels: none -> 155 us  [the longest x3 126 us: remote(): pl.pallas_call(functools.partial(kernel, sizes), out_shape=outs, in_specs...]
    ppermute x36 -> x0, starting transfers between devices: 95.2 us -> none  [the longest x18 71.8 us: padded(): lax.ppermute(lax.slice_in_dim(block, block.shape[dim] - width, None, axis...]
    another operation x3 -> x0, loops' own time: 47.9 us -> none  [the longest x1 21.3 us: query_back(): lax.map(query_per_head, jnp.arange(H, dtype=jnp.int32))]
    unnamed x77 -> x13, local copies, waits for them, and re-layouts: 35.4 us -> 4.91 us
    dynamic_slice x56 -> x0, local copies, waits for them, and re-layouts: 20.7 us -> none  [the longest x24 19.3 us: attend_forward(): lax.map(attend_per_head, jnp.arange(H, dtype=jnp.int32))]
  transfers between devices with their start and end apart: 38 -> 0, of which waited for: 15 -> 0; matrix products, arithmetic and copies ran while one was open for 7% -> 0% of each run, Pallas kernels for 0% -> 0%
where the time goes in v1:
time: 176 us; the launch traced here: 175 us
  Pallas kernels  155 us (88%)
  other arithmetic  10.2 us (6%)
  local copies, waits for them, and re-layouts  5.65 us (3%)
  between operations  1.99 us (1%)
  matrix products  1.96 us (1%)
    pallas_call x3, Pallas kernels, remote(): pl.pallas_call(functools.partial(kernel, sizes), out_shape=outs, in_specs...  126 us
    pallas_call x1, Pallas kernels, attend(): pl.pallas_call(attend_kernel, grid=(groups,), out_shape=(shape((P_SIZE, D...  28.8 us
    unnamed x13, local copies, waits for them, and re-layouts  4.91 us

profile of v1, /device:TPU:0, one launch (start us, length us, event | category | flops | bytes accessed | tf_op | source)
XLA Modules:
  0.0 174.9 jit_solution(4722347254912661285)
XLA Ops:
  1.9 0.7 reduce
  2.7 0.7 broadcast_in_dim.46.bias_ref
  3.4 1.8 %bitcast_select_fusion.gin = bf16[256,512]{1,0:T(8,128)(2,1)} fusion(bf16[1,1,1,256,512]{4,3,2,1,0:T(8,128)(2,1)} %param.19, pred[256]{0:T(512)(128)(4,1)S(1)} %iota_compare_fusion), kind=kLoop, calls=%fused_computation.6 | loop fusion | flops 131072 | bytes 524544 | tf_op jit(solution)/shard_map/jit(_where)/select_n | solution.py:480
  5.1 1.5 broadcast_select_fusion
  6.6 62.7 %shard_map.145 = (bf16[256,512]{1,0:T(8,128)(2,1)}, bf16[256,512]{1,0:T(8,128)(2,1)}, bf16[1792,1152]{1,0:T(8,128)(2,1)}, bf16[2,2,4,2,32,1024]{5,4,3,2,1,0:T(8,128)(2,1)}) custom-call(bf16[256,512]{1,0:T(8,128)(2,1)} %bitcast.34, bf16[256,128]{1,0:T(8,128)(2,1)} %broadcast_in_dim.46.bias_ref, bf16[512,512]{1,0:T(8,128)(2,1)} %wq.3, bf16[512,1024]{1,0:T(8,128)(2,1)} %wkv.3, ...), custom_call_target="tpu_custom_call" | custom-call | tf_op jit(solution)/shard_map/pallas_call | solution.py:406
  69.3 0.0 copy-start
  69.3 28.8 %shard_map.146 = (bf16[256,512]{1,0:T(8,128)(2,1)}, bf16[256,512]{1,0:T(8,128)(2,1)}, bf16[1792,512]{1,0:T(8,128)(2,1)}, bf16[1792,512]{1,0:T(8,128)(2,1)}, bf16...) custom-call(s32[6]{0:T(128)} %bitcast.44, bf16[256,512]{1,0:T(8,128)(2,1)} %get-tuple-element.20.q_ref, ...), custom_call_target="tpu_custom_call" | custom-call | tf_op jit(solution)/shard_map/pallas_call | solution.py:423
  98.1 0.0 copy-done
  98.1 2.0 %fusion.1 = bf16[1,1,1,256,512]{4,3,2,1,0:T(8,128)(2,1)} fusion(bf16[256,512]{1,0:T(8,128)(2,1)} %get-tuple-element.24.attn, bf16[512,512]{1,0:T(8,128)(2,1)S(1)} %copy-done, pred[256]{0:T(512)(128)(4,1)S(1)} %iota_compare_fusion), kind=kOutput, calls=%fused_computation.5 | convolution fusion | flops 134479872 | bytes 1048832 | tf_op jit(solution)/shard_map/dot_general | solution.py:39
  100.1 3.1 %pad_maximum_fusion = bf16[1024,1024]{1,0:T(8,128)(2,1)} fusion(bf16[1024,512]{1,0:T(8,128)(2,1)} %get-tuple-element.29, bf16[1024,512]{1,0:T(8,128)(2,1)} %get-tuple-element.28), kind=kLoop, calls=%fused_computation | loop fusion | flops 4194304 | bytes 4194304 | tf_op jit(solution)/shard_map/concatenate | solution.py:505
  103.2 38.0 %shard_map.147 = (bf16[256,512]{1,0:T(8,128)(2,1)}, bf16[512,1024]{1,0:T(8,128)(2,1)}, bf16[512,1024]{1,0:T(8,128)(2,1)}, f32[32,1024]{1,0:T(8,128)}) custom-call(bf16[256,512]{1,0:T(8,128)(2,1)} %bitcast.35, bf16[512,512]{1,0:T(8,128)(2,1)} %wq.3, bf16[512,1024]{1,0:T(8,128)(2,1)} %wkv.3, bf16[256,512]{1,0:T(8,128)(2,1)} %bitcast_select_fusion.gin, ...), custom_call_target="tpu_custom_call" | custom-call | tf_op jit(solution)/shard_map/pallas_call | solution.py:406
  141.2 3.1 %pad_maximum_fusion.1.source = bf16[2,2,4,2,32,1024]{5,4,3,2,1,0:T(8,128)(2,1)} fusion(bf16[2,2,4,2,16,1024]{5,4,3,2,1,0:T(8,128)(2,1)} %bitcast.37, bf16[2,2,4,2,16,1024]{5,4,3,2,1,0:T(8,128)(2,1)} %bitcast.36), kind=kLoop, calls=%fused_computation.1 | loop fusion | flops 4194304 | bytes 4194304 | tf_op jit(solution)/shard_map/concatenate | solution.py:523
  144.3 0.0 copy-start.2
  144.3 0.0 copy-start.1
  144.3 25.7 %shard_map.148 = f32[32,1024]{1,0:T(8,128)} custom-call(bf16[2,2,4,2,32,1024]{5,4,3,2,1,0:T(8,128)(2,1)} %pad_maximum_fusion.1.source), custom_call_target="tpu_custom_call" | custom-call | tf_op jit(solution)/shard_map/pallas_call | solution.py:406
  170.0 0.8 slice_bitcast_fusion
  170.9 0.8 slice_bitcast_fusion.1
  171.7 0.6 copy.18
  172.3 0.6 copy.17
  172.9 0.6 copy.16
  173.5 0.0 copy-done.2
  173.5 0.7 copy.19
  174.2 0.0 copy-done.1
  174.2 0.7 copy.23
  (2 shorter events, 0.0 us)
Async XLA Ops:
  69.3 28.8 %copy-start = (bf16[512,512]{1,0:T(8,128)(2,1)S(1)}, bf16[512,512]{1,0:T(8,128)(2,1)}, u32[]{:S(2)}) copy-start(bf16[512,512]{1,0:T(8,128)(2,1)} %wo.1) | copy-start | bytes 1572868
  144.3 29.2 %copy-start.2 = (f32[32,1024]{1,0:T(8,128)S(1)}, f32[32,1024]{1,0:T(8,128)}, u32[]{:S(2)}) copy-start(f32[32,1024]{1,0:T(8,128)} %get-tuple-element.33) | copy-start | bytes 393220
  144.3 29.9 %copy-start.1 = (bf16[256,512]{1,0:T(8,128)(2,1)S(1)}, bf16[256,512]{1,0:T(8,128)(2,1)}, u32[]{:S(2)}) copy-start(bf16[256,512]{1,0:T(8,128)(2,1)} %get-tuple-element.30) | copy-start | bytes 786436

commit v2 on v1

--- a/solution.py
+++ b/solution.py
@@ -156,13 +156,13 @@
             )
         return found
 
-    def start(self, level):
-        for half in range(2):
+    def start(self, level, halves=(0, 1)):
+        for half in halves:
             for copy in self.copies(half, level):
                 copy.start()
 
-    def finish(self, level, out=None):
-        for half in range(2):
+    def finish(self, level, out=None, halves=(0, 1)):
+        for half in halves:
             at = half * 4 + level
             for copy in self.copies(half, level):
                 copy.wait()
@@ -225,21 +225,24 @@
 
     scatter.finish(0)
     scatter.start(1)
-    for face, (there, _) in enumerate(faces):
-        @pl.when(there)
-        def _(face=face):
-            face_copy(face, face ^ 1).start()
-
-        @pl.when(jnp.logical_not(there))
-        def _(face=face):
-            keys[(1 + face) * P_SIZE : (2 + face) * P_SIZE, :] = jnp.zeros((P_SIZE, AUG), BF16)
-
+    def send_faces(wanted):
+        for face in wanted:
+            @pl.when(faces[face][0])
+            def _(face=face):
+                face_copy(face, face ^ 1).start()
+
+            @pl.when(jnp.logical_not(faces[face][0]))
+            def _(face=face):
+                keys[(1 + face) * P_SIZE : (2 + face) * P_SIZE, :] = jnp.zeros((P_SIZE, AUG), BF16)
+
+    send_faces((2, 3))
     q_out[...] = nn(normed_low, wq[...]).astype(BF16)
     g_out[...] = nt(gin[...], wo[...]).astype(BF16)
     scatter.finish(1)
     scatter.start(2)
     scatter.finish(2)
     scatter.start(3)
+    send_faces((0, 1, 4, 5))
     scatter.finish(3, piece)
     final[place.pos["y"], place.pos["c"], place.pos["gy"], place.pos["gz"]] = piece[...]
     for level in (3, 2, 1, 0):
@@ -394,6 +397,102 @@
         scatter.finish(level, out if level == 3 else None)
 
 
+def finish_kernel(sizes, count, rows_ref, wq, wkv, wo, gin, attn, gq, dk, dv, dbk, dbv,
+                  update_out, grad_out, base_out, sum_out, rk, rv, base, weights, *scratch):
+    base_refs, weight_refs, (ss, rs) = scratch[:11], scratch[11:22], scratch[22:]
+    gx, gy, gz = sizes
+    devices = gx * gy * gz
+    half = PIECE // 2
+    place = Place(sizes)
+    place.barrier()
+    faces = place.faces()
+
+    def spread(target, rows, columns, values):
+        step = values.shape[0] // devices
+        for d in range(devices):
+            x, y, z = d // (gy * gz), d // gz % gy, d % gz
+            target[x // 2, x % 2, y, z, rows, columns] = values[d * step : (d + 1) * step]
+
+    def face_copy(face, slot, which):
+        source, target = ((dk, rk), (dv, rv))[which]
+        return pltpu.make_async_remote_copy(
+            src_ref=source.at[pl.ds((1 + face) * P_SIZE, P_SIZE)],
+            dst_ref=target.at[slot],
+            send_sem=ss.at[2 * face + which],
+            recv_sem=rs.at[2 * slot + which],
+            device_id=faces[face][1],
+            device_id_type=MESH,
+        )
+
+    for face, (there, _) in enumerate(faces):
+        @pl.when(there)
+        def _(face=face):
+            face_copy(face, face ^ 1, 0).start()
+            face_copy(face, face ^ 1, 1).start()
+
+        @pl.when(jnp.logical_not(there))
+        def _(face=face):
+            rk[face] = jnp.zeros((P_SIZE, D), BF16)
+            rv[face] = jnp.zeros((P_SIZE, D), BF16)
+
+    both, lower, upper = slice(0, PIECE), slice(0, half), slice(half, PIECE)
+    left, right = slice(0, D), slice(D, 2 * D)
+    spread(base, both, left, dbk[...])
+    spread(base, both, right, dbv[...])
+    first = Scatter(place, base, base_refs)
+    second = Scatter(place, weights, weight_refs)
+    first.start(0)
+    normed, inv_std = layer_norm(rows_ref[...].astype(F32))
+    normed_low = normed.astype(BF16)
+    spread(weights, upper, left, tn(normed_low, gq[...]).astype(BF16))
+    spread(weights, upper, right, tn(attn[...], gin[...]).astype(BF16))
+    second.start(0, (1,))
+    first.finish(0)
+    first.start(1)
+    slot = lax.broadcasted_iota(jnp.int32, (P_SIZE, D), 0)
+    projected = nn(attn[...], wo[...])
+    update_out[...] = jnp.where(slot < count[0], projected, 0.0).astype(BF16)
+    second.finish(0, None, (1,))
+    second.start(1, (1,))
+    for face, (there, _) in enumerate(faces):
+        @pl.when(there)
+        def _(face=face):
+            for which in range(2):
+                face_copy(face, face ^ 1, which).wait_send()
+                face_copy(face, face, which).wait_recv()
+    sum_k = dk[0:P_SIZE, :].astype(F32)
+    sum_v = dv[0:P_SIZE, :].astype(F32)
+    for face in range(6):
+        sum_k = sum_k + rk[face].astype(F32)
+        sum_v = sum_v + rv[face].astype(F32)
+    pair_k = sum_k.astype(BF16)
+    pair_v = sum_v.astype(BF16)
+    spread(weights, lower, left, tn(normed_low, pair_k).astype(BF16))
+    spread(weights, lower, right, tn(normed_low, pair_v).astype(BF16))
+    second.start(0, (0,))
+    first.finish(1)
+    first.start(2)
+    second.finish(1, None, (1,))
+    second.start(2, (1,))
+    second.finish(0, None, (0,))
+    second.start(1, (0,))
+    grad = nt(gq[...], wq[...]) + nt(pair_k, wkv[:, :D]) + nt(pair_v, wkv[:, D:])
+    first_mean = jnp.mean(grad, axis=-1, keepdims=True)
+    second_mean = jnp.mean(grad * normed, axis=-1, keepdims=True)
+    grad_out[...] = (inv_std * (grad - first_mean - normed * second_mean)).astype(BF16)
+    first.finish(2)
+    first.start(3)
+    second.finish(2, None, (1,))
+    second.start(3, (1,))
+    second.finish(1, None, (0,))
+    second.start(2, (0,))
+    first.finish(3, base_out)
+    second.finish(3, sum_out, (1,))
+    second.finish(2, None, (0,))
+    second.start(3, (0,))
+    second.finish(3, sum_out, (0,))
+
+
 def vmem():
     return pl.BlockSpec(memory_space=pltpu.VMEM)
 
@@ -402,11 +501,12 @@
     return jax.ShapeDtypeStruct(dims, dtype)
 
 
-def remote(kernel, sizes, outs, scratch, collective, operands):
+def remote(kernel, sizes, outs, scratch, collective, operands, scalars=0):
     return pl.pallas_call(
         functools.partial(kernel, sizes),
         out_shape=outs,
-        in_specs=[vmem()] * len(operands),
+        in_specs=[pl.BlockSpec(memory_space=pltpu.SMEM)] * scalars
+        + [vmem()] * (len(operands) - scalars),
         out_specs=jax.tree.map(lambda _: vmem(), outs),
         scratch_shapes=scratch,
         compiler_params=pltpu.CompilerParams(
@@ -500,30 +600,61 @@
     )
     baffle = final.reshape(NB, 2 * D)
     attn, gq, dk, dv, dbk, dbv = attend(pattern[0, 0, 0], q, g, keys, baffle)
-    projected = nn(attn, output_weight)
-    update = jnp.where(valid_rows[:, None], projected, 0.0).astype(BF16)
-    base = jnp.concatenate([dbk, dbv], axis=1).reshape(pieces)
-    grad_rows, w_kv, w_qo, base_sum = remote(
-        return_kernel,
-        sizes,
-        (
-            shape((P_SIZE, D), BF16),
-            shape((D, 2 * D), BF16),
-            shape((D, 2 * D), BF16),
-            shape((PIECE, width), F32),
-        ),
-        [pltpu.VMEM((6, P_SIZE, D), BF16), pltpu.VMEM((6, P_SIZE, D), BF16)]
-        + scatter_scratch(sizes, width)
-        + [dma((12,)), dma((12,))],
-        1,
-        (rows_in, query_weight, key_value_weight, grad_in, attn, gq, dk, dv, base),
-    )
+    halos = [pltpu.VMEM((6, P_SIZE, D), BF16), pltpu.VMEM((6, P_SIZE, D), BF16)]
+    face_sems = [dma((12,)), dma((12,))]
     if width == 2 * D:
         half = PIECE // 2
-        weights = jnp.concatenate(
-            [w_kv.reshape(devices, half, width), w_qo.reshape(devices, half, width)], axis=1
+        update, grad_rows, base_sum, weight_sum = remote(
+            finish_kernel,
+            sizes,
+            (
+                shape((P_SIZE, D), BF16),
+                shape((P_SIZE, D), BF16),
+                shape((PIECE, width), F32),
+                shape((PIECE, width), F32),
+            ),
+            halos
+            + [pltpu.VMEM(pieces, BF16), pltpu.VMEM(pieces, BF16)]
+            + scatter_scratch(sizes, width)
+            + scatter_scratch(sizes, width)
+            + face_sems,
+            1,
+            (
+                counts[0, 0],
+                rows_in,
+                query_weight,
+                key_value_weight,
+                output_weight,
+                grad_in,
+                attn,
+                gq,
+                dk,
+                dv,
+                dbk,
+                dbv,
+            ),
+            1,
         )
+        grad_kv = weight_sum[:half].reshape(-1)
+        grad_q = weight_sum[half:, :D].reshape(-1)
+        grad_o = weight_sum[half:, D:].reshape(-1)
     else:
+        projected = nn(attn, output_weight)
+        update = jnp.where(valid_rows[:, None], projected, 0.0).astype(BF16)
+        base = jnp.concatenate([dbk, dbv], axis=1).reshape(pieces)
+        grad_rows, w_kv, w_qo, base_sum = remote(
+            return_kernel,
+            sizes,
+            (
+                shape((P_SIZE, D), BF16),
+                shape((D, 2 * D), BF16),
+                shape((D, 2 * D), BF16),
+                shape((PIECE, width), F32),
+            ),
+            halos + scatter_scratch(sizes, width) + face_sems,
+            2,
+            (rows_in, query_weight, key_value_weight, grad_in, attn, gq, dk, dv, base),
+        )
         weights = jnp.concatenate(
             [
                 w_kv.reshape(devices, -1),
@@ -532,19 +663,14 @@
             ],
             axis=1,
         )
-    weight_sum = remote(
-        scatter_kernel,
-        sizes,
-        shape((PIECE, width), F32),
-        scatter_scratch(sizes, width),
-        2,
-        (weights.reshape(pieces),),
-    )
-    if width == 2 * D:
-        grad_kv = weight_sum[:half].reshape(-1)
-        grad_q = weight_sum[half:, :D].reshape(-1)
-        grad_o = weight_sum[half:, D:].reshape(-1)
-    else:
+        weight_sum = remote(
+            scatter_kernel,
+            sizes,
+            shape((PIECE, width), F32),
+            scatter_scratch(sizes, width),
+            3,
+            (weights.reshape(pieces),),
+        )
         flat = weight_sum.reshape(-1)
         part = D * D // devices
         grad_kv, grad_q, grad_o = flat[: 2 * part], flat[2 * part : 3 * part], flat[3 * part :]

time: 176 us -> 145 us (0.82)
  Pallas kernels: 155 us -> 129 us
  other arithmetic: 10.2 us -> 3.95 us
  local copies, waits for them, and re-layouts: 5.65 us -> 9.17 us
  matrix products: 1.96 us -> 0 us
    pallas_call x3 -> x2, Pallas kernels: 126 us -> 100 us  [remote(): pl.pallas_call(functools.partial(kernel, sizes), out_shape=outs, in_specs...]
    concatenate x2 -> x0, other arithmetic: 6.28 us -> none  [the longest x1 3.15 us: body(): jnp.concatenate([w_kv.reshape(devices, half, width), w_qo.reshape(devices...]
    unnamed x13 -> x8, local copies, waits for them, and re-layouts: 4.91 us -> 8.44 us
    dot_general x1 -> x0, matrix products: 1.96 us -> none  [nn(): return jnp.dot(left, right, preferred_element_type=F32)]
where the time goes in v2:
time: 145 us; the launch traced here: 144 us
  Pallas kernels  129 us (89%)
  local copies, waits for them, and re-layouts  9.17 us (6%)
  other arithmetic  3.95 us (3%)
  between operations  1.96 us (1%)
    pallas_call x2, Pallas kernels, remote(): pl.pallas_call(functools.partial(kernel, sizes), out_shape=outs, in_specs...  100 us
    pallas_call x1, Pallas kernels, attend(): pl.pallas_call(attend_kernel, grid=(groups,), out_shape=(shape((P_SIZE, D...  28.6 us
    unnamed x8, local copies, waits for them, and re-layouts  8.44 us

profile of v2, /device:TPU:0, one launch (start us, length us, event | category | flops | bytes accessed | tf_op | source)
XLA Modules:
  0.0 143.7 jit_solution(1944974244829276932)
XLA Ops:
  1.9 0.7 reduce
  2.6 0.7 broadcast_in_dim.36.bias_ref
  3.4 1.8 %bitcast_select_fusion.gin = bf16[256,512]{1,0:T(8,128)(2,1)} fusion(bf16[1,1,1,256,512]{4,3,2,1,0:T(8,128)(2,1)} %param.19, pred[256]{0:T(512)(128)(4,1)S(1)} %iota_compare_fusion), kind=kLoop, calls=%fused_computation.1 | loop fusion | flops 131072 | bytes 524544 | tf_op jit(solution)/shard_map/jit(_where)/select_n | solution.py:580
  5.1 1.5 %broadcast_select_fusion = bf16[1,1024,1024]{2,1,0:T(8,128)(2,1)} fusion(bf16[1,1024,1024]{2,1,0:T(8,128)(2,1)} %param.17, pred[]{:T(512)S(6)} %eq.3), kind=kLoop, calls=%fused_computation | loop fusion | flops 1048576 | bytes 4194305 | tf_op jit(solution)/shard_map/jit(_where)/select_n | solution.py:584
  6.6 53.7 %shard_map.145 = (bf16[256,512]{1,0:T(8,128)(2,1)}, bf16[256,512]{1,0:T(8,128)(2,1)}, bf16[1792,1152]{1,0:T(8,128)(2,1)}, bf16[2,2,4,2,32,1024]{5,4,3,2,1,0:T(8,128)(2,1)}) custom-call(bf16[256,512]{1,0:T(8,128)(2,1)} %bitcast.29, bf16[256,128]{1,0:T(8,128)(2,1)} %broadcast_in_dim.36.bias_ref, bf16[512,512]{1,0:T(8,128)(2,1)} %wq.3, bf16[512,1024]{1,0:T(8,128)(2,1)} %wkv.3, ...), custom_call_target="tpu_custom_call" | custom-call | tf_op jit(solution)/shard_map/pallas_call | solution.py:505
  60.3 28.6 %shard_map.146 = (bf16[256,512]{1,0:T(8,128)(2,1)}, bf16[256,512]{1,0:T(8,128)(2,1)}, bf16[1792,512]{1,0:T(8,128)(2,1)}, bf16[1792,512]{1,0:T(8,128)(2,1)}, bf16...) custom-call(s32[6]{0:T(128)} %bitcast.38, bf16[256,512]{1,0:T(8,128)(2,1)} %get-tuple-element.20.q_ref, ...), custom_call_target="tpu_custom_call" | custom-call | tf_op jit(solution)/shard_map/pallas_call | solution.py:523
  88.9 46.4 %shard_map.147 = (bf16[256,512]{1,0:T(8,128)(2,1)}, bf16[256,512]{1,0:T(8,128)(2,1)}, f32[32,1024]{1,0:T(8,128)}, f32[32,1024]{1,0:T(8,128)}) custom-call(s32[1]{0:T(128)} %bitcast.22.count, bf16[256,512]{1,0:T(8,128)(2,1)} %bitcast.30, bf16[512,512]{1,0:T(8,128)(2,1)} %wq.3, bf16[512,1024]{1,0:T(8,128)(2,1)} %wkv.3, bf16[512,512]{1,0:T(8,128)(2,1)} %wo.3, ...), custom_call_target="tpu_custom_call" | custom-call | tf_op jit(solution)/shard_map/pallas_call | solution.py:505
  135.3 0.8 slice_bitcast_fusion
  136.1 0.8 slice_bitcast_fusion.1
  136.9 0.6 copy.18
  137.5 0.6 copy.17
  138.2 0.6 copy.16
  138.8 1.6 %copy.19 = f32[4,8,8,128]{3,1,2,0:T(8,128)} copy(f32[4,8,8,128]{3,2,1,0:T(8,128)} %bitcast.33) | data formatting | bytes 262144
  140.4 1.7 %copy.24 = bf16[1,1,1,256,512]{4,3,2,1,0:T(8,128)(2,1)} copy(bf16[1,1,1,256,512]{4,3,2,1,0:T(8,128)(2,1)} %bitcast.32) | data formatting | bytes 524288
  142.0 1.7 %copy.25 = bf16[1,1,1,256,512]{4,3,2,1,0:T(8,128)(2,1)} copy(bf16[1,1,1,256,512]{4,3,2,1,0:T(8,128)(2,1)} %bitcast.31) | data formatting | bytes 524288
  (2 shorter events, 0.0 us)

commit v3 on v2

--- a/solution.py
+++ b/solution.py
@@ -90,8 +90,8 @@
 ORDERS = (("c", "gz", "y", "gy"), ("c", "y", "gz", "gy"))
 
 
-def select(fixed, rows):
-    return tuple(fixed.get(axis, slice(None)) for axis in AXES) + (rows, slice(None))
+def select(fixed, rows, columns=slice(None)):
+    return tuple(fixed.get(axis, slice(None)) for axis in AXES) + (rows, columns)
 
 
 def stage_plan(sizes):
@@ -117,8 +117,9 @@
 
 
 class Scatter:
-    def __init__(self, place, source, scratch):
+    def __init__(self, place, source, scratch, columns=slice(None)):
         self.place = place
+        self.columns = columns
         self.source = source
         self.recv = scratch[:8]
         self.work, self.send_sem, self.recv_sem = scratch[8:11]
@@ -139,6 +140,7 @@
         at = half * 4 + level
         axis, n = self.plan[at][1], self.plan[at][2]
         origin = self.source if level == 0 else self.work
+        columns = self.columns if level == 0 else slice(None)
         found = []
         for step in range(1, n):
             target = lax.rem(self.place.pos[axis] + step, n)
@@ -146,7 +148,7 @@
             fixed[axis] = target
             found.append(
                 pltpu.make_async_remote_copy(
-                    src_ref=origin.at[select(fixed, self.rows(half))],
+                    src_ref=origin.at[select(fixed, self.rows(half), columns)],
                     dst_ref=self.recv[at].at[step - 1],
                     send_sem=self.send_sem.at[self.offsets[at] + step - 1],
                     recv_sem=self.recv_sem.at[self.offsets[at] + step - 1],
@@ -168,46 +170,62 @@
                 copy.wait()
             origin = self.source if level == 0 else self.work
             where = select(self.fixed(half, level + 1), self.rows(half))
-            total = origin[where].astype(F32)
+            taken = where[:-1] + ((self.columns if level == 0 else slice(None)),)
+            total = origin[taken].astype(F32)
             for step in range(self.plan[at][2] - 1):
                 total = total + self.recv[at][step].astype(F32)
             if out is None:
                 self.work[where] = total.astype(BF16)
             else:
-                out[self.rows(half), :] = total.astype(out.dtype)
-
-
-def gather_copies(place, final, send_sem, recv_sem, level):
+                out[self.rows(half), self.columns] = total.astype(out.dtype)
+
+    def advance(self, level, halves=(0, 1)):
+        for half in halves:
+            self.finish(level, None, (half,))
+            self.start(level + 1, (half,))
+
+
+def gather_copies(place, final, send_sem, recv_sem, level, group, half, columns):
     counts, plan = stage_plan(place.sizes)
+    order = ORDERS[half]
+    axis = order[level]
+    base = sum(n - 1 for _, _, n, _ in plan[: half * 4 + level])
+    base += group * sum(n - 1 for _, _, n, _ in plan)
+    fixed = {a: place.pos[a] for a in order[: level + 1]}
+    view = final.at[select(fixed, pl.ds(half * (PIECE // 2), PIECE // 2), columns)]
     found = []
-    for half in range(2):
-        order = ORDERS[half]
-        axis = order[level]
-        base = sum(n - 1 for h, a, n, _ in plan[: half * 4 + level])
-        fixed = {a: place.pos[a] for a in order[: level + 1]}
-        view = final.at[select(fixed, pl.ds(half * (PIECE // 2), PIECE // 2))]
-        for step in range(1, counts[axis]):
-            target = lax.rem(place.pos[axis] + step, counts[axis])
-            found.append(
-                pltpu.make_async_remote_copy(
-                    src_ref=view,
-                    dst_ref=view,
-                    send_sem=send_sem.at[base + step - 1],
-                    recv_sem=recv_sem.at[base + step - 1],
-                    device_id=place.device(axis, target),
-                    device_id_type=MESH,
-                )
+    for step in range(1, counts[axis]):
+        target = lax.rem(place.pos[axis] + step, counts[axis])
+        found.append(
+            pltpu.make_async_remote_copy(
+                src_ref=view,
+                dst_ref=view,
+                send_sem=send_sem.at[base + step - 1],
+                recv_sem=recv_sem.at[base + step - 1],
+                device_id=place.device(axis, target),
+                device_id_type=MESH,
             )
+        )
     return found
+
+
+def groups_of(width):
+    return 2 if width % (2 * LANES) == 0 else 1
 
 
 def project_kernel(sizes, rows_ref, bias_ref, wq, wkv, wo, gin, baf, q_out, g_out, keys, final,
                    *scratch):
-    scatter_refs, (gs, gr, hs, hr, piece) = scratch[:11], scratch[11:]
+    width = baf.shape[-1]
+    groups = groups_of(width)
+    gs, gr, hs, hr = scratch[11 * groups :]
     place = Place(sizes)
     place.barrier()
-    scatter = Scatter(place, baf, scatter_refs)
-    scatter.start(0)
+    columns = [slice(g * (width // groups), (g + 1) * (width // groups)) for g in range(groups)]
+    scatters = [
+        Scatter(place, baf, scratch[11 * g : 11 * g + 11], columns[g]) for g in range(groups)
+    ]
+    for scatter in scatters:
+        scatter.start(0)
     normed_low = layer_norm(rows_ref[...].astype(F32))[0].astype(BF16)
     keys[0:P_SIZE, 0 : 2 * D] = nn(normed_low, wkv[...]).astype(BF16)
     keys[0:P_SIZE, 2 * D : AUG] = bias_ref[...]
@@ -223,8 +241,9 @@
             device_id_type=MESH,
         )
 
-    scatter.finish(0)
-    scatter.start(1)
+    for scatter in scatters:
+        scatter.advance(0)
+
     def send_faces(wanted):
         for face in wanted:
             @pl.when(faces[face][0])
@@ -238,19 +257,27 @@
     send_faces((2, 3))
     q_out[...] = nn(normed_low, wq[...]).astype(BF16)
     g_out[...] = nt(gin[...], wo[...]).astype(BF16)
-    scatter.finish(1)
-    scatter.start(2)
-    scatter.finish(2)
-    scatter.start(3)
+    for level in (1, 2):
+        for scatter in scatters:
+            scatter.advance(level)
     send_faces((0, 1, 4, 5))
-    scatter.finish(3, piece)
-    final[place.pos["y"], place.pos["c"], place.pos["gy"], place.pos["gz"]] = piece[...]
+    mine = final.at[place.pos["y"], place.pos["c"], place.pos["gy"], place.pos["gz"]]
+    streams = [(g, half) for g in range(groups) for half in range(2)]
+
+    def spread_copies(level, g, half):
+        return gather_copies(place, final, gs, gr, level, g, half, columns[g])
+
+    for g, half in streams:
+        scatters[g].finish(3, mine, (half,))
+        for copy in spread_copies(3, g, half):
+            copy.start()
     for level in (3, 2, 1, 0):
-        sent = gather_copies(place, final, gs, gr, level)
-        for copy in sent:
-            copy.start()
-        for copy in sent:
-            copy.wait()
+        for g, half in streams:
+            for copy in spread_copies(level, g, half):
+                copy.wait()
+            if level > 0:
+                for copy in spread_copies(level - 1, g, half):
+                    copy.start()
     for face, (there, _) in enumerate(faces):
         @pl.when(there)
         def _(face=face):
@@ -258,8 +285,8 @@
             face_copy(face, face).wait_recv()
 
 
-def attend_kernel(flags, q_ref, g_ref, k_ref, v_ref, b_ref, bk_ref, bv_ref,
-                  attn_ref, gq_ref, dk_ref, dv_ref, dbk_ref, dbv_ref, e_scr, p_scr, d_scr):
+def attend_kernel(flags, count, q_ref, g_ref, k_ref, v_ref, b_ref, bk_ref, bv_ref, wo_ref,
+                  update_ref, attn_ref, gq_ref, dk_ref, dv_ref, dbk_ref, dbv_ref, e_scr, p_scr, u_scr):
     lane = lax.broadcasted_iota(jnp.int32, (P_SIZE, PAIR), 1)
     zero = jnp.zeros((P_SIZE, PAIR), BF16)
     q = q_ref[...] * jnp.asarray(1.0 / math.sqrt(HD), BF16)
@@ -303,7 +330,24 @@
         p_scr[span, :] = p
         attn_t = attn_t + tn(values[rows, :], p)
     picked = jnp.concatenate([attn_t[:HD, :P_SIZE], attn_t[HD:, P_SIZE:]], axis=0)
-    attn_ref[...] = picked.T.astype(BF16)
+    attn = picked.T.astype(BF16)
+    attn_ref[...] = attn
+    step = pl.program_id(0)
+    projected = nn(attn, wo_ref[...])
+
+    @pl.when(step == 0)
+    def _():
+        u_scr[...] = projected
+
+    @pl.when(step > 0)
+    def _():
+        u_scr[...] += projected
+
+    @pl.when(step == D // PAIR - 1)
+    def _():
+        slot = lax.broadcasted_iota(jnp.int32, (P_SIZE, D), 0)
+        update_ref[...] = jnp.where(slot < count[0], u_scr[...], 0.0).astype(BF16)
+
     product = g.astype(F32).T * picked.astype(BF16).astype(F32)
     row_dot = jnp.concatenate(
         [
@@ -397,8 +441,8 @@
         scatter.finish(level, out if level == 3 else None)
 
 
-def finish_kernel(sizes, count, rows_ref, wq, wkv, wo, gin, attn, gq, dk, dv, dbk, dbv,
-                  update_out, grad_out, base_out, sum_out, rk, rv, base, weights, *scratch):
+def finish_kernel(sizes, rows_ref, wq, wkv, gin, attn, gq, dk, dv, dbk, dbv,
+                  grad_out, base_out, sum_out, rk, rv, base, weights, *scratch):
     base_refs, weight_refs, (ss, rs) = scratch[:11], scratch[11:22], scratch[22:]
     gx, gy, gz = sizes
     devices = gx * gy * gz
@@ -447,13 +491,8 @@
     spread(weights, upper, left, tn(normed_low, gq[...]).astype(BF16))
     spread(weights, upper, right, tn(attn[...], gin[...]).astype(BF16))
     second.start(0, (1,))
-    first.finish(0)
-    first.start(1)
-    slot = lax.broadcasted_iota(jnp.int32, (P_SIZE, D), 0)
-    projected = nn(attn[...], wo[...])
-    update_out[...] = jnp.where(slot < count[0], projected, 0.0).astype(BF16)
-    second.finish(0, None, (1,))
-    second.start(1, (1,))
+    first.advance(0)
+    second.advance(0, (1,))
     for face, (there, _) in enumerate(faces):
         @pl.when(there)
         def _(face=face):
@@ -470,26 +509,19 @@
     spread(weights, lower, left, tn(normed_low, pair_k).astype(BF16))
     spread(weights, lower, right, tn(normed_low, pair_v).astype(BF16))
     second.start(0, (0,))
-    first.finish(1)
-    first.start(2)
-    second.finish(1, None, (1,))
-    second.start(2, (1,))
-    second.finish(0, None, (0,))
-    second.start(1, (0,))
+    first.advance(1)
+    second.advance(1, (1,))
+    second.advance(0, (0,))
     grad = nt(gq[...], wq[...]) + nt(pair_k, wkv[:, :D]) + nt(pair_v, wkv[:, D:])
     first_mean = jnp.mean(grad, axis=-1, keepdims=True)
     second_mean = jnp.mean(grad * normed, axis=-1, keepdims=True)
     grad_out[...] = (inv_std * (grad - first_mean - normed * second_mean)).astype(BF16)
-    first.finish(2)
-    first.start(3)
-    second.finish(2, None, (1,))
-    second.start(3, (1,))
-    second.finish(1, None, (0,))
-    second.start(2, (0,))
+    first.advance(2)
+    second.advance(2, (1,))
+    second.advance(1, (0,))
     first.finish(3, base_out)
     second.finish(3, sum_out, (1,))
-    second.finish(2, None, (0,))
-    second.start(3, (0,))
+    second.advance(2, (0,))
     second.finish(3, sum_out, (0,))
 
 
@@ -501,12 +533,11 @@
     return jax.ShapeDtypeStruct(dims, dtype)
 
 
-def remote(kernel, sizes, outs, scratch, collective, operands, scalars=0):
+def remote(kernel, sizes, outs, scratch, collective, operands):
     return pl.pallas_call(
         functools.partial(kernel, sizes),
         out_shape=outs,
-        in_specs=[pl.BlockSpec(memory_space=pltpu.SMEM)] * scalars
-        + [vmem()] * (len(operands) - scalars),
+        in_specs=[vmem()] * len(operands),
         out_specs=jax.tree.map(lambda _: vmem(), outs),
         scratch_shapes=scratch,
         compiler_params=pltpu.CompilerParams(
@@ -515,7 +546,7 @@
     )(*operands)
 
 
-def attend(flags, q, g, keys, baffle):
+def attend(flags, count, q, g, keys, baffle, output_weight):
     def cols(rows, shift):
         return pl.BlockSpec((rows, PAIR), lambda p: (0, p + shift))
 
@@ -524,6 +555,7 @@
         attend_kernel,
         grid=(groups,),
         out_shape=(
+            shape((P_SIZE, D), BF16),
             shape((P_SIZE, D), BF16),
             shape((P_SIZE, D), BF16),
             shape((NEAR, D), BF16),
@@ -533,6 +565,7 @@
         ),
         in_specs=[
             pl.BlockSpec(memory_space=pltpu.SMEM),
+            pl.BlockSpec(memory_space=pltpu.SMEM),
             cols(P_SIZE, 0),
             cols(P_SIZE, 0),
             cols(NEAR, 0),
@@ -540,8 +573,10 @@
             pl.BlockSpec((NEAR, PAIR), lambda p: (0, 2 * groups)),
             cols(NB, 0),
             cols(NB, groups),
+            pl.BlockSpec((PAIR, D), lambda p: (p, 0)),
         ],
         out_specs=(
+            pl.BlockSpec((P_SIZE, D), lambda p: (0, 0)),
             cols(P_SIZE, 0),
             cols(P_SIZE, 0),
             cols(NEAR, 0),
@@ -552,10 +587,10 @@
         scratch_shapes=[
             pltpu.VMEM((ALL, 2 * P_SIZE), F32),
             pltpu.VMEM((ALL, 2 * P_SIZE), BF16),
-            pltpu.VMEM((8, LANES), BF16),
+            pltpu.VMEM((P_SIZE, D), F32),
         ],
         compiler_params=pltpu.CompilerParams(vmem_limit_bytes=VMEM_BYTES),
-    )(flags, q, g, keys, keys, keys, baffle, baffle)
+    )(flags, count, q, g, keys, keys, keys, baffle, baffle, output_weight)
 
 
 def body(
@@ -582,7 +617,8 @@
     width = NB * 2 * D // (devices * PIECE)
     pieces = (gx // 2, 2, gy, gz, PIECE, width)
     store = jnp.where(me == owner_device[0], baffle_store[0], jnp.zeros((), BF16)).reshape(pieces)
-    copies = sum(n - 1 for _, _, n, _ in stage_plan(sizes)[1])
+    groups = groups_of(width)
+    copies = groups * sum(n - 1 for _, _, n, _ in stage_plan(sizes)[1])
     dma = pltpu.SemaphoreType.DMA
     q, g, keys, final = remote(
         project_kernel,
@@ -593,22 +629,23 @@
             shape((NEAR, AUG), BF16),
             shape(pieces, BF16),
         ),
-        scatter_scratch(sizes, width)
-        + [dma((copies,)), dma((copies,)), dma((6,)), dma((6,)), pltpu.VMEM((PIECE, width), BF16)],
+        scatter_scratch(sizes, width // groups) * groups
+        + [dma((copies,)), dma((copies,)), dma((6,)), dma((6,))],
         0,
         (rows_in, bias_lanes, query_weight, key_value_weight, output_weight, grad_in, store),
     )
     baffle = final.reshape(NB, 2 * D)
-    attn, gq, dk, dv, dbk, dbv = attend(pattern[0, 0, 0], q, g, keys, baffle)
+    update, attn, gq, dk, dv, dbk, dbv = attend(
+        pattern[0, 0, 0], counts[0, 0], q, g, keys, baffle, output_weight
+    )
     halos = [pltpu.VMEM((6, P_SIZE, D), BF16), pltpu.VMEM((6, P_SIZE, D), BF16)]
     face_sems = [dma((12,)), dma((12,))]
     if width == 2 * D:
         half = PIECE // 2
-        update, grad_rows, base_sum, weight_sum = remote(
+        grad_rows, base_sum, weight_sum = remote(
             finish_kernel,
             sizes,
             (
-                shape((P_SIZE, D), BF16),
                 shape((P_SIZE, D), BF16),
                 shape((PIECE, width), F32),
                 shape((PIECE, width), F32),
@@ -620,11 +657,9 @@
             + face_sems,
             1,
             (
-                counts[0, 0],
                 rows_in,
                 query_weight,
                 key_value_weight,
-                output_weight,
                 grad_in,
                 attn,
                 gq,
@@ -633,14 +668,11 @@
                 dbk,
                 dbv,
             ),
-            1,
         )
         grad_kv = weight_sum[:half].reshape(-1)
         grad_q = weight_sum[half:, :D].reshape(-1)
         grad_o = weight_sum[half:, D:].reshape(-1)
     else:
-        projected = nn(attn, output_weight)
-        update = jnp.where(valid_rows[:, None], projected, 0.0).astype(BF16)
         base = jnp.concatenate([dbk, dbv], axis=1).reshape(pieces)
         grad_rows, w_kv, w_qo, base_sum = remote(
             return_kernel,

time: 145 us -> 142 us (0.979)
  local copies, waits for them, and re-layouts: 9.17 us -> 7.5 us
    pallas_call x2, Pallas kernels: 100 us -> 97.2 us  [remote(): pl.pallas_call(functools.partial(kernel, sizes), out_shape=outs, in_specs...]
    pallas_call x1, Pallas kernels: 28.6 us -> 31.3 us  [attend(): pl.pallas_call(attend_kernel, grid=(groups,), out_shape=(shape((P_SIZE, D...]
    unnamed x8 -> x7, local copies, waits for them, and re-layouts: 8.44 us -> 6.77 us
where the time goes in v3:
time: 142 us
  Pallas kernels  129 us (91%)
  local copies, waits for them, and re-layouts  7.5 us (5%)
  other arithmetic  3.95 us (3%)
  between operations  1.96 us (1%)
    pallas_call x2, Pallas kernels, remote(): pl.pallas_call(functools.partial(kernel, sizes), out_shape=outs, in_specs...  97.2 us
    pallas_call x1, Pallas kernels, attend(): pl.pallas_call(attend_kernel, grid=(groups,), out_shape=(shape((P_SIZE, D...  31.3 us
    unnamed x7, local copies, waits for them, and re-layouts  6.77 us

profile of v3, /device:TPU:0, one launch (start us, length us, event | category | flops | bytes accessed | tf_op | source)
XLA Modules:
  0.0 141.9 jit_solution(6431513863649556211)
XLA Ops:
  1.9 0.7 reduce
  2.6 0.7 broadcast_in_dim.34.bias_ref
  3.4 1.8 %bitcast_select_fusion.gin = bf16[256,512]{1,0:T(8,128)(2,1)} fusion(bf16[1,1,1,256,512]{4,3,2,1,0:T(8,128)(2,1)} %param.19, pred[256]{0:T(512)(128)(4,1)S(1)} %iota_compare_fusion), kind=kLoop, calls=%fused_computation.1 | loop fusion | flops 131072 | bytes 524544 | tf_op jit(solution)/shard_map/jit(_where)/select_n | solution.py:615
  5.1 1.5 %broadcast_select_fusion = bf16[1,1024,1024]{2,1,0:T(8,128)(2,1)} fusion(bf16[1,1024,1024]{2,1,0:T(8,128)(2,1)} %param.17, pred[]{:T(512)S(6)} %eq.3), kind=kLoop, calls=%fused_computation | loop fusion | flops 1048576 | bytes 4194305 | tf_op jit(solution)/shard_map/jit(_where)/select_n | solution.py:619
  6.6 49.8 %shard_map.145 = (bf16[256,512]{1,0:T(8,128)(2,1)}, bf16[256,512]{1,0:T(8,128)(2,1)}, bf16[1792,1152]{1,0:T(8,128)(2,1)}, bf16[2,2,4,2,32,1024]{5,4,3,2,1,0:T(8,128)(2,1)}) custom-call(bf16[256,512]{1,0:T(8,128)(2,1)} %bitcast.29, bf16[256,128]{1,0:T(8,128)(2,1)} %broadcast_in_dim.34.bias_ref, bf16[512,512]{1,0:T(8,128)(2,1)} %wq.3, bf16[512,1024]{1,0:T(8,128)(2,1)} %wkv.3, ...), custom_call_target="tpu_custom_call" | custom-call | tf_op jit(solution)/shard_map/pallas_call | solution.py:537
  56.4 31.3 %shard_map.146 = (bf16[256,512]{1,0:T(8,128)(2,1)}, bf16[256,512]{1,0:T(8,128)(2,1)}, bf16[256,512]{1,0:T(8,128)(2,1)}, bf16[1792,512]{1,0:T(8,128)(2,1)}, bf16[...) custom-call(s32[6]{0:T(128)} %bitcast.37, s32[1]{0:T(128)} %bitcast.22.count, ...), custom_call_target="tpu_custom_call" | custom-call | tf_op jit(solution)/shard_map/pallas_call | solution.py:554
  87.7 47.5 %shard_map.147 = (bf16[256,512]{1,0:T(8,128)(2,1)}, f32[32,1024]{1,0:T(8,128)}, f32[32,1024]{1,0:T(8,128)}) custom-call(bf16[256,512]{1,0:T(8,128)(2,1)} %bitcast.30, bf16[512,512]{1,0:T(8,128)(2,1)} %wq.3, bf16[512,1024]{1,0:T(8,128)(2,1)} %wkv.3, bf16[256,512]{1,0:T(8,128)(2,1)} %bitcast_select_fusion.gin, bf16[256,512]{1,0:T(8,128)(2,1)} %get-tuple-element.25.attn, ...), custom_call_target="tpu_custom_call" | custom-call | tf_op jit(solution)/shard_map/pallas_call | solution.py:537
  135.1 1.6 %copy.19 = f32[4,8,8,128]{3,1,2,0:T(8,128)} copy(f32[4,8,8,128]{3,2,1,0:T(8,128)} %bitcast.33) | data formatting | bytes 262144
  136.7 0.8 slice_bitcast_fusion
  137.6 0.8 slice_bitcast_fusion.1
  138.3 0.6 copy.18
  139.0 0.6 copy.17
  139.6 0.6 copy.16
  140.2 1.7 %copy.23 = bf16[1,1,1,256,512]{4,3,2,1,0:T(8,128)(2,1)} copy(bf16[1,1,1,256,512]{4,3,2,1,0:T(8,128)(2,1)} %bitcast.31) | data formatting | bytes 524288
  (2 shorter events, 0.0 us)

commit v4 on v3

--- a/solution.py
+++ b/solution.py
@@ -493,6 +493,7 @@
     second.start(0, (1,))
     first.advance(0)
     second.advance(0, (1,))
+    first.advance(1)
     for face, (there, _) in enumerate(faces):
         @pl.when(there)
         def _(face=face):
@@ -509,7 +510,6 @@
     spread(weights, lower, left, tn(normed_low, pair_k).astype(BF16))
     spread(weights, lower, right, tn(normed_low, pair_v).astype(BF16))
     second.start(0, (0,))
-    first.advance(1)
     second.advance(1, (1,))
     second.advance(0, (0,))
     grad = nt(gq[...], wq[...]) + nt(pair_k, wkv[:, :D]) + nt(pair_v, wkv[:, D:])

time: 142 us -> 142 us (level)
  no operation moved by 1% of the time
where the time goes in v4:
time: 142 us
  Pallas kernels  128 us (90%)
  local copies, waits for them, and re-layouts  7.5 us (5%)
  other arithmetic  3.95 us (3%)
  between operations  1.96 us (1%)
    pallas_call x2, Pallas kernels, remote(): pl.pallas_call(functools.partial(kernel, sizes), out_shape=outs, in_specs...  97.2 us
    pallas_call x1, Pallas kernels, attend(): pl.pallas_call(attend_kernel, grid=(groups,), out_shape=(shape((P_SIZE, D...  31.3 us
    unnamed x7, local copies, waits for them, and re-layouts  6.77 us

profile of v4, /device:TPU:0, one launch (start us, length us, event | category | flops | bytes accessed | tf_op | source)
XLA Modules:
  0.0 141.9 jit_solution(6440816323380108399)
XLA Ops:
  1.9 0.7 reduce
  2.6 0.7 broadcast_in_dim.34.bias_ref
  3.4 1.8 %bitcast_select_fusion.gin = bf16[256,512]{1,0:T(8,128)(2,1)} fusion(bf16[1,1,1,256,512]{4,3,2,1,0:T(8,128)(2,1)} %param.19, pred[256]{0:T(512)(128)(4,1)S(1)} %iota_compare_fusion), kind=kLoop, calls=%fused_computation.1 | loop fusion | flops 131072 | bytes 524544 | tf_op jit(solution)/shard_map/jit(_where)/select_n | solution.py:615
  5.1 1.5 %broadcast_select_fusion = bf16[1,1024,1024]{2,1,0:T(8,128)(2,1)} fusion(bf16[1,1024,1024]{2,1,0:T(8,128)(2,1)} %param.17, pred[]{:T(512)S(6)} %eq.3), kind=kLoop, calls=%fused_computation | loop fusion | flops 1048576 | bytes 4194305 | tf_op jit(solution)/shard_map/jit(_where)/select_n | solution.py:619
  6.6 50.1 %shard_map.145 = (bf16[256,512]{1,0:T(8,128)(2,1)}, bf16[256,512]{1,0:T(8,128)(2,1)}, bf16[1792,1152]{1,0:T(8,128)(2,1)}, bf16[2,2,4,2,32,1024]{5,4,3,2,1,0:T(8,128)(2,1)}) custom-call(bf16[256,512]{1,0:T(8,128)(2,1)} %bitcast.29, bf16[256,128]{1,0:T(8,128)(2,1)} %broadcast_in_dim.34.bias_ref, bf16[512,512]{1,0:T(8,128)(2,1)} %wq.3, bf16[512,1024]{1,0:T(8,128)(2,1)} %wkv.3, ...), custom_call_target="tpu_custom_call" | custom-call | tf_op jit(solution)/shard_map/pallas_call | solution.py:537
  56.7 31.3 %shard_map.146 = (bf16[256,512]{1,0:T(8,128)(2,1)}, bf16[256,512]{1,0:T(8,128)(2,1)}, bf16[256,512]{1,0:T(8,128)(2,1)}, bf16[1792,512]{1,0:T(8,128)(2,1)}, bf16[...) custom-call(s32[6]{0:T(128)} %bitcast.37, s32[1]{0:T(128)} %bitcast.22.count, ...), custom_call_target="tpu_custom_call" | custom-call | tf_op jit(solution)/shard_map/pallas_call | solution.py:554
  88.0 47.1 %shard_map.147 = (bf16[256,512]{1,0:T(8,128)(2,1)}, f32[32,1024]{1,0:T(8,128)}, f32[32,1024]{1,0:T(8,128)}) custom-call(bf16[256,512]{1,0:T(8,128)(2,1)} %bitcast.30, bf16[512,512]{1,0:T(8,128)(2,1)} %wq.3, bf16[512,1024]{1,0:T(8,128)(2,1)} %wkv.3, bf16[256,512]{1,0:T(8,128)(2,1)} %bitcast_select_fusion.gin, bf16[256,512]{1,0:T(8,128)(2,1)} %get-tuple-element.25.attn, ...), custom_call_target="tpu_custom_call" | custom-call | tf_op jit(solution)/shard_map/pallas_call | solution.py:537
  135.1 1.6 %copy.19 = f32[4,8,8,128]{3,1,2,0:T(8,128)} copy(f32[4,8,8,128]{3,2,1,0:T(8,128)} %bitcast.33) | data formatting | bytes 262144
  136.7 0.8 slice_bitcast_fusion
  137.6 0.8 slice_bitcast_fusion.1
  138.3 0.6 copy.18
  139.0 0.6 copy.17
  139.6 0.6 copy.16
  140.2 1.7 %copy.23 = bf16[1,1,1,256,512]{4,3,2,1,0:T(8,128)(2,1)} copy(bf16[1,1,1,256,512]{4,3,2,1,0:T(8,128)(2,1)} %bitcast.31) | data formatting | bytes 524288
  (2 shorter events, 0.0 us)
